TPU v7x, 512 devices: a whole 4x4x16 slice. The times are simulated.
512 devices in a mesh: gx: 32 (over x_lo, z), gy: 16 (over x_hi, y, core).
Axes of the slice: x: 4 (x_hi: 2, x_lo: 2; x = x_hi * 2 + x_lo), y: 4, z: 16, core: 2. Of those that a mesh axis runs over, the one named last changes fastest.
Arguments:
- hidden_in: bfloat16 [2048, 16384], P('gy', 'gx'), may hold values from -200 to 200
- norm_gain: float32 [16384], P('gx'), may hold values from 0.1 to 1.9
- w_query: bfloat16 [16384, 8192], P('gx', 'gy'), may hold values from -24 to 24
- w_key: bfloat16 [16384, 1024], P('gx'), may hold values from -1 to 1
- w_value: bfloat16 [16384, 1024], P('gx'), may hold values from -0.046875 to 0.046875
- w_out: bfloat16 [8192, 16384], P('gy', 'gx'), may hold values from -0.06591797 to 0.06591797
- seg_lengths: int32 [8], replicated, may hold values from 1 to 512, 2048 in all
Outputs:
- update: bfloat16 [2048, 16384], P('gy', 'gx')
Inputs may be any that keep to these rules, and one draw needn't show every extreme that they name: `seg_lengths`: the 8 lengths sum to 2048 and the longest is exactly 512.
All inputs are finite; a program needn't handle non-finite values.
Results may differ from a plain program's by a relative error of at most 0.04.
Values may be sent and summed in bfloat16 or wider, within the bound.
A program may use at most 64 MiB of HBM per device.

v0:
```python
import math

import jax
import jax.numpy as jnp
from jax import lax
from jax.sharding import PartitionSpec as P

H = 64
KVH = 8
HD = 128


ROPE_BASE = 500000.0
EPS = 1e-05


def rotate(values, position, head_size):
    half = head_size // 2
    exponent = jnp.arange(half, dtype=jnp.float32) * (2.0 / head_size)
    frequency = ROPE_BASE ** (-exponent)
    angle = position[:, None, None] * frequency[None, None, :]
    cosine = jnp.cos(angle)
    sine = jnp.sin(angle)
    first = values[..., :half]
    second = values[..., half:]
    return jnp.concatenate(
        [first * cosine - second * sine, second * cosine + first * sine], axis=-1
    )


def segment_table(seg_lengths, tokens):
    ends = jnp.cumsum(seg_lengths)
    starts = ends - seg_lengths
    index = jnp.arange(tokens, dtype=jnp.int32)
    member = ((index[:, None] >= starts[None, :]) & (index[:, None] < ends[None, :])).astype(
        jnp.int32
    )
    seg_id = jnp.sum(member * jnp.arange(seg_lengths.shape[0], dtype=jnp.int32)[None, :], axis=1)
    first_index = jnp.sum(member * starts[None, :], axis=1)
    return (seg_id, index - first_index)


def normalize(block, gain, squares, model_width):
    widened = block.astype(jnp.float32)
    scale = lax.rsqrt(squares / model_width + EPS)
    return (widened * scale[:, None] * gain[None, :]).astype(jnp.bfloat16)


def shards(hidden_in, norm_gain, w_query, w_key, w_value, w_out, seg_lengths):
    rows_own, width = hidden_in.shape
    model_width = width * lax.axis_size("gx")
    tokens = rows_own * lax.axis_size("gy")
    query_rows = tokens // lax.axis_size("gx")
    widened = hidden_in.astype(jnp.float32)
    squares = lax.psum(jnp.sum(widened * widened, axis=1), "gx")
    source = normalize(hidden_in, norm_gain, squares, model_width)
    gathered = lax.all_gather(source, "gy", axis=0, tiled=True)
    query_cols = w_query.shape[1]
    heads_local = query_cols // HD
    group = H // KVH
    kv_local = max(1, heads_local // group)
    pair_cols = kv_local * HD
    first_head = lax.axis_index("gy") * heads_local // group
    key_own = lax.dynamic_slice_in_dim(w_key, first_head * HD, pair_cols, 1)
    value_own = lax.dynamic_slice_in_dim(w_value, first_head * HD, pair_cols, 1)
    seg_id, position = segment_table(seg_lengths, tokens)
    here = lax.axis_index("gx") * query_rows
    query_seg = lax.dynamic_slice_in_dim(seg_id, here, query_rows)
    query_pos = lax.dynamic_slice_in_dim(position, here, query_rows)
    query_index = here + jnp.arange(query_rows, dtype=jnp.int32)
    query_sum = lax.psum_scatter(
        jnp.dot(gathered, w_query, preferred_element_type=jnp.float32).astype(jnp.bfloat16),
        "gx",
        scatter_dimension=0,
        tiled=True,
    ).astype(jnp.float32)
    pair_part = jnp.concatenate(
        [
            jnp.dot(gathered, key_own, preferred_element_type=jnp.float32),
            jnp.dot(gathered, value_own, preferred_element_type=jnp.float32),
        ],
        axis=1,
    )
    pair_sum = lax.psum(pair_part.astype(jnp.bfloat16), "gx").astype(jnp.float32)
    key_raw = pair_sum[:, :pair_cols].astype(jnp.bfloat16)
    value_raw = pair_sum[:, pair_cols:].astype(jnp.bfloat16)
    group_local = heads_local // kv_local
    queries = rotate(
        query_sum.reshape(query_rows, heads_local, HD), query_pos.astype(jnp.float32), HD
    ).astype(jnp.bfloat16)
    queries = queries.reshape(query_rows, kv_local, group_local, HD)
    key_count = key_raw.shape[0]
    keys = rotate(
        key_raw.astype(jnp.float32).reshape(key_count, kv_local, HD),
        position.astype(jnp.float32),
        HD,
    )
    keys = keys.astype(jnp.bfloat16).reshape(key_count, pair_cols)
    score_scale = 1.0 / math.sqrt(HD)
    running = jnp.full((kv_local, group_local, query_rows), -1e30, jnp.float32)
    count = keys.shape[0]
    key_index = jnp.arange(count, dtype=jnp.int32)
    allowed = (query_seg[:, None] == seg_id[None, :]) & (key_index[None, :] <= query_index[:, None])
    key_heads = keys.reshape(count, kv_local, HD)
    value_heads = value_raw.reshape(count, kv_local, HD)
    scores = (
        jnp.einsum("rkgd,nkd->kgrn", queries, key_heads, preferred_element_type=jnp.float32)
        * score_scale
    )
    scores = jnp.where(allowed[None, None], scores, -1e30)
    newest = jnp.maximum(running, jnp.max(scores, axis=-1))
    weights = jnp.where(allowed[None, None], jnp.exp(scores - newest[..., None]), 0.0)
    denominator = jnp.sum(weights, axis=-1)
    added = jnp.einsum(
        "kgrn,nkd->rkgd",
        weights.astype(jnp.bfloat16),
        value_heads,
        preferred_element_type=jnp.float32,
    )
    accum = added
    running, denominator, accum = (newest, denominator, accum)
    attended = (
        (accum / denominator.transpose(2, 0, 1)[..., None])
        .reshape(query_rows, query_cols)
        .astype(jnp.bfloat16)
    )
    partial_out = jnp.dot(
        lax.all_gather(attended, "gx", axis=0, tiled=True),
        w_out,
        preferred_element_type=jnp.float32,
    )
    return lax.psum_scatter(partial_out.astype(jnp.bfloat16), "gy", scatter_dimension=0, tiled=True)


def solution(mesh):
    in_specs = (
        P("gy", "gx"),
        P("gx"),
        P("gx", "gy"),
        P("gx", None),
        P("gx", None),
        P("gy", "gx"),
        P(),
    )
    out_specs = P("gy", "gx")
    return jax.shard_map(shards, mesh=mesh, in_specs=in_specs, out_specs=out_specs, check_vma=False)
```

profile of v0, /device:TPU:1, one launch (start us, length us, event | category | flops | bytes accessed | tf_op | source)
XLA Modules:
  0.0 757.2 jit_solution(15568946854750830513)
XLA Ops:
  6.5 0.0 copy-start
  6.5 0.0 all-gather.3.cloned.1.call-start
  6.5 1.1 fusion.23
  7.6 57.2 %psum.14 = f32[128]{0:T(128)S(1)} all-reduce(f32[128]{0:T(128)S(1)} %fusion.23), channel_id=1, replica_groups=mesh['gx'=32,'gy'=16] {'gx'}, use_global_device_ids=true, to_apply=%region_1.0 | all-reduce | flops 128 | bytes 1024 | tf_op jit(solution)/shard_map/psum | solution.py:55
  64.9 1.7 fusion.25
  66.5 0.0 all-gather.3.cloned.1.call-update
  66.6 0.0 all-reduce.2.cloned.1.call-start
  66.6 68.3 %all-gather.3.cloned.1.call-done = bf16[2048,512]{1,0:T(8,128)(2,1)} async-done(((bf16[128,512]{1,0:T(8,128)(2,1)}), bf16[2048,512]{1,0:T(8,128)(2,1)}) %all-gather.3.cloned.1.call-update) | async-done | bytes 2097168 | tf_op jit(solution)/shard_map/all_gather | solution.py:57
  134.9 0.0 copy-done
  134.9 0.0 copy-start.1
  134.9 2.6 convolution_convert_fusion.2
  137.5 0.0 copy-done.1
  137.5 1.7 convolution_convert_fusion.3
  139.2 1.1 pad_maximum_fusion
  140.3 0.0 all-reduce.2.cloned.1.call-update
  140.3 0.0 reduce-scatter.3.cloned.1.call-start
  140.3 3.6 convolution_convert_fusion.1
  144.0 0.0 copy-start.4
  144.0 0.0 reduce-scatter.3.cloned.1.call-update
  144.0 0.0 all-gather.5.cloned.1.call-start
  144.1 0.6 copy-done.4
  144.6 0.2 reduce-window.8
  144.8 0.1 select_reduce_fusion
  144.9 0.1 dynamic_slice.14
  145.1 0.1 dynamic-slice_convert_fusion
  145.1 0.2 multiply_cosine_fusion.1
  145.3 0.2 fusion.22
  145.6 230.3 %all-reduce.2.cloned.1.call-done = bf16[2048,256]{0,1:T(8,128)(2,1)} async-done(((bf16[2048,256]{0,1:T(8,128)(2,1)}), bf16[2048,256]{0,1:T(8,128)(2,1)}) %all-reduce.2.cloned.1.call-update) | async-done | bytes 1048592 | tf_op jit(solution)/shard_map/psum | solution.py:84
  375.8 1.1 fusion.19
  377.0 2.3 fusion.27
  379.3 129.1 %reduce-scatter.3.cloned.1.call-done = bf16[64,512]{1,0:T(8,128)(2,1)} async-done(((bf16[2048,512]{1,0:T(8,128)(2,1)}), bf16[64,512]{1,0:T(8,128)(2,1)}) %reduce-scatter.3.cloned.1.call-update) | async-done | bytes 65552 | tf_op jit(solution)/shard_map/reduce_scatter | solution.py:71
  508.4 0.9 reshape.307
  509.2 0.1 fusion.39
  509.4 0.0 copy-start.2
  509.4 0.6 fusion.40
  510.1 0.5 fusion.2
  510.6 0.0 copy-start.3
  510.6 0.0 copy-done.2
  510.7 0.5 fusion.5
  511.2 0.1 copy.21
  511.2 0.6 copy.34
  511.9 0.0 all-gather.5.cloned.1.call-update
  511.9 0.0 reduce-scatter.5.cloned.1.call-start
  511.9 127.9 %all-gather.5.cloned.1.call-done = bf16[2048,512]{1,0:T(8,128)(2,1)} async-done(((bf16[64,512]{1,0:T(8,128)(2,1)}), bf16[2048,512]{1,0:T(8,128)(2,1)}) %all-gather.5.cloned.1.call-update) | async-done | bytes 2097168 | tf_op jit(solution)/shard_map/all_gather | solution.py:128
  639.8 0.0 copy-done.3
  639.8 4.1 convolution_convert_fusion
  644.0 0.0 reduce-scatter.5.cloned.1.call-update
  644.0 106.7 %reduce-scatter.5.cloned.1.call-done = bf16[128,512]{1,0:T(8,128)(2,1)} async-done(((bf16[2048,512]{1,0:T(8,128)(2,1)}), bf16[128,512]{1,0:T(8,128)(2,1)}) %reduce-scatter.5.cloned.1.call-update) | async-done | bytes 131088 | tf_op jit(solution)/shard_map/reduce_scatter | solution.py:132
  (7 shorter events, 0.1 us)
Async XLA Ops:
  6.5 128.4 %copy-start = (bf16[512,1024]{1,0:T(8,128)(2,1)S(1)}, bf16[512,1024]{1,0:T(8,128)(2,1)}, u32[]{:S(2)}) copy-start(bf16[512,1024]{1,0:T(8,128)(2,1)} %param.11) | copy-start | bytes 3145732
  6.5 128.4 %all-gather.3.cloned.1.call-start = ((), (), s32[]{:S(2)}) async-start(), calls=%async_computation.2 | async-start | bytes 2228224 | tf_op jit(solution)/shard_map/all_gather | solution.py:57
  66.6 309.3 %all-reduce.2.cloned.1.call-start = ((), (), s32[]{:S(2)}) async-start(), calls=%async_computation.3 | async-start | bytes 2097152 | tf_op jit(solution)/shard_map/psum | solution.py:84
  134.9 2.6 copy-start.1
  140.3 368.1 %reduce-scatter.3.cloned.1.call-start = ((), (), s32[]{:S(2)}) async-start(), calls=%async_computation.4 | async-start | bytes 2162688 | tf_op jit(solution)/shard_map/reduce_scatter | solution.py:71
  144.0 0.7 copy-start.4
  144.0 495.8 %all-gather.5.cloned.1.call-start = ((), (), s32[]{:S(2)}) async-start(), calls=%async_computation.5 | async-start | bytes 2162688 | tf_op jit(solution)/shard_map/all_gather | solution.py:128
  509.4 1.2 copy-start.2
  510.6 129.2 %copy-start.3 = (bf16[512,512]{1,0:T(8,128)(2,1)S(1)}, bf16[512,512]{1,0:T(8,128)(2,1)}, u32[]{:S(2)}) copy-start(bf16[512,512]{1,0:T(8,128)(2,1)} %param.12) | copy-start | bytes 1572868
  511.9 238.8 %reduce-scatter.5.cloned.1.call-start = ((), (), s32[]{:S(2)}) async-start(), calls=%async_computation.6 | async-start | bytes 2228224 | tf_op jit(solution)/shard_map/reduce_scatter | solution.py:132
Sparse Core Ops, SparseCore 0:
  66.7 68.1 all-gather.2
  140.4 235.3 all-reduce.1
  378.9 129.4 reduce-scatter.2
  512.0 127.7 all-gather.4
  644.4 106.1 reduce-scatter.4
where the time goes:
time: 758 us; the launch traced here: 757 us
  waiting for transfers between devices  662 us (87%)
  blocking collectives  57.2 us (8%)
  between operations  13.3 us (2%)
  matrix products  13.2 us (2%)
  other arithmetic  8.63 us (1%)
    psum x1, waiting for transfers between devices, shards(): lax.psum(pair_part.astype(jnp.bfloat16), 'gx').astype(jnp.float32)  230 us
    reduce_scatter x1, waiting for transfers between devices, shards(): lax.psum_scatter(jnp.dot(gathered, w_query, preferred_element_type=jnp.fl...  129 us
    all_gather x1, waiting for transfers between devices, shards(): lax.all_gather(attended, 'gx', axis=0, tiled=True)  128 us
    reduce_scatter x1, waiting for transfers between devices, shards(): lax.psum_scatter(partial_out.astype(jnp.bfloat16), 'gy', scatter_dimensio...  107 us
    all_gather x1, waiting for transfers between devices, shards(): gathered = lax.all_gather(source, 'gy', axis=0, tiled=True)  68.3 us
    psum x1, blocking collectives, shards(): squares = lax.psum(jnp.sum(widened * widened, axis=1), 'gx')  57.2 us
  transfers between devices with their start and end apart: 5, of which 5 were waited for; matrix products, arithmetic and copies ran while one was open for 1% of the time, Pallas kernels for 0%

commit v1 on v0

v1 whole, which is shorter than its diff:
```python
import math

import jax
import jax.numpy as jnp
from jax import lax
from jax.experimental import pallas as pl
from jax.experimental.pallas import tpu as pltpu
from jax.sharding import PartitionSpec as P

MESH = pl.DeviceIdType.MESH
HD = 128
HALF = HD // 2
SEGS = 8
ROPE_BASE = 500000.0
EPS = 1e-05
BF = jnp.bfloat16
F32 = jnp.float32

NZ = 16
TB = 128
TH = 64
WIDTH = 512
QF = 256
XF = HD + QF
ZF = WIDTH - QF
MSG = XF + 2 * ZF
RS = 32
WIN = 5
KEYS = WIN * TB
MODEL = 16384


def body(h, gain, wq, wk, wv, wo, seg, out, *s):
    (
        gath, wraw, kvraw, wcat, wov, gv, part, xs, xr, zs, zr, sq, sqs, sqr, sqx, fxs, fxr, kvw, af, al, cs, cr, own, es, er, el, ex,
        in_sem, ga_s, ga_r, x_s, x_r, z_s, z_r, q_s, q_r, f_s, f_r, kz_s, kx_s, kc_s, k_r,
        dz_s, dx_s, d_r, c_s, c_r, e_s, e_r, ex_s, ex_r,
    ) = s
    gx = lax.axis_index("gx")
    gy = lax.axis_index("gy")
    xlo, z = lax.div(gx, NZ), lax.rem(gx, NZ)
    xhi, y, core = lax.div(gy, 8), lax.rem(lax.div(gy, 2), 4), lax.rem(gy, 2)
    xot, hot, cot = 1 - xlo, 1 - xhi, 1 - core

    def zm(v):
        return lax.rem(v + NZ, NZ)

    def ym(v):
        return lax.rem(v + 4, 4)

    def at_z(d):
        return {"gx": xlo * NZ + zm(z + d), "gy": gy}

    def at_y(yy):
        return {"gx": gx, "gy": xhi * 8 + yy * 2 + core}

    dev_x = {"gx": xot * NZ + z, "gy": gy}
    dev_h = {"gx": gx, "gy": hot * 8 + y * 2 + core}
    dev_c = {"gx": gx, "gy": xhi * 8 + y * 2 + cot}

    def rc(src, dst, ss, rs, dev):
        return pltpu.make_async_remote_copy(src_ref=src, dst_ref=dst, send_sem=ss, recv_sem=rs, device_id=dev, device_id_type=MESH)

    barrier = pltpu.get_barrier_semaphore()
    greet = [dev_x, dev_h, dev_c] + [at_y(ym(y + d)) for d in (1, 2, 3)] + [at_z(d) for d in (1, 2, 3, 4, -1, -2, -3, -4)]
    for d in greet:
        pl.semaphore_signal(barrier, inc=1, device_id=d, device_id_type=MESH)
    head = pl.multiple_of((xhi * 4 + y) * HD, HD)
    cp_h = pltpu.make_async_copy(h, gath.at[gy], in_sem.at[0])
    cp_q = pltpu.make_async_copy(wq, wraw, in_sem.at[1])
    cp_o = pltpu.make_async_copy(wo, wov, in_sem.at[2])
    cp_g = pltpu.make_async_copy(gain, gv, in_sem.at[3])
    cp_k = pltpu.make_async_copy(wk.at[:, pl.ds(head, HD)], kvraw.at[0], in_sem.at[4])
    cp_v = pltpu.make_async_copy(wv.at[:, pl.ds(head, HD)], kvraw.at[1], in_sem.at[5])
    loads = [cp_h, cp_q, cp_o, cp_g, cp_k, cp_v]
    for c in loads:
        c.start()
    pl.semaphore_wait(barrier, len(greet))

    def gather_copy(blk, dev, n, src=None):
        return rc(gath.at[blk] if src is None else src, gath.at[blk], ga_s.at[n], ga_r.at[blk], dev)

    sends = []

    def go(c):
        c.start()
        sends.append(c)

    def blk(hh, yy, cc):
        return hh * 8 + yy * 2 + cc

    go(gather_copy(gy, dev_h, 0, h))
    for n, d in enumerate((1, 3, 2)):
        go(gather_copy(gy, at_y(ym(y + d)), 1 + n, h))
    go(gather_copy(gy, dev_c, 4, h))

    for c in loads:
        c.wait()
    gcol = jnp.transpose(jnp.broadcast_to(gv[...], (HD, WIDTH)))
    is_core0 = core == 0
    kv_w = jnp.where(is_core0, kvraw[0].astype(F32), kvraw[1].astype(F32))
    wcat[:, 0:HD] = (kv_w * gcol).astype(BF)
    for j in range(WIDTH // HD):
        wcat[:, HD * (j + 1) : HD * (j + 2)] = (wraw[:, HD * j : HD * (j + 1)].astype(F32) * gcol).astype(BF)

    far = blk(hot, y, core)
    gather_copy(far, dev_h, 0).wait_recv()
    for n, d in enumerate((1, 3, 2)):
        go(gather_copy(far, at_y(ym(y + d)), 5 + n))
    go(gather_copy(far, dev_c, 8))
    for n, d in enumerate((1, 3, 2)):
        for m, hh in enumerate((xhi, hot)):
            b = blk(hh, ym(y + d), core)
            gather_copy(b, dev_c, 9 + 2 * n + m).wait_recv()
            go(gather_copy(b, dev_c, 9 + 2 * n + m))
    for hh in (xhi, hot):
        for d in range(4):
            gather_copy(blk(hh, ym(y + d), cot), dev_c, 0).wait_recv()

    ones = jnp.ones((8, WIDTH), BF)
    nt = (((1,), (1,)), ((), ()))
    mine_top = xlo == 0

    def x_copy(b):
        return rc(xs.at[b], xr.at[b], x_s.at[b], x_r.at[b], dev_x)

    def z_copy(d, k, r):
        rows = pl.ds(r * RS, RS)
        return rc(zs.at[d, k, rows], zr.at[d, k, rows], z_s.at[d, k, r], z_r.at[d, k, r], at_z(1 - 2 * d))

    def q_copy(d, k):
        return rc(sqs.at[d, k], sqr.at[d, k], q_s.at[d, k], q_r.at[d, k], at_z(1 - 2 * d))

    def product(b):
        x = gath[b]
        res = jnp.dot(x, wcat[...], preferred_element_type=F32).astype(BF)
        top, bot = res[0:TH], res[TH:TB]
        part[b, :, 0:XF] = jnp.where(mine_top, top[:, 0:XF], bot[:, 0:XF])
        xs[b] = jnp.where(mine_top, bot[:, 0:XF], top[:, 0:XF])
        x_copy(b).start()
        part[b, :, XF : XF + ZF] = top[:, XF:]
        part[b, :, XF + ZF : MSG] = bot[:, XF:]
        xf = x.astype(F32)
        x2 = xf * xf
        hi = x2.astype(BF)
        lo = (x2 - hi.astype(F32)).astype(BF)
        sq[b] = lax.dot_general(ones, hi, nt, preferred_element_type=F32) + lax.dot_general(ones, lo, nt, preferred_element_type=F32)

    def own_rows(b, r):
        rows = slice(r * RS, r * RS + RS)
        a = part[b, rows, 0:XF].astype(F32) + xr[b, rows, :].astype(F32)
        return jnp.concatenate([a, part[b, rows, XF:MSG].astype(F32)], axis=1)

    def ring_step(d, k, b):
        x_copy(b).wait_recv()
        for r in range(2):
            rows = slice(r * RS, r * RS + RS)

            @pl.when(k == 0)
            def _():
                zs[d, k, rows, :] = own_rows(b, r).astype(BF)

            @pl.when(k > 0)
            def _():
                z_copy(d, k - 1, r).wait_recv()
                zs[d, k, rows, :] = (own_rows(b, r) + zr[d, k - 1, rows, :].astype(F32)).astype(BF)

            z_copy(d, k, r).start()

        @pl.when(k == 0)
        def _():
            sqs[d, k] = sq[b]

        @pl.when(k > 0)
        def _():
            q_copy(d, k - 1).wait_recv()
            sqs[d, k] = sq[b] + sqr[d, k - 1]

        q_copy(d, k).start()

    def reduce_step(i, _):
        @pl.when(i < 8)
        def _():
            product(zm(z + 8 - i))
            product(zm(z - 7 + i))

        @pl.when(i > 0)
        def _():
            ring_step(0, i - 1, zm(z + 9 - i))

        @pl.when((i > 0) & (i < 8))
        def _():
            ring_step(1, i - 1, zm(z - 8 + i))

        return 0

    lax.fori_loop(0, 9, reduce_step, 0)

    def firsts(tq):
        start = jnp.zeros_like(tq)
        total = jnp.int32(0)
        for i in range(SEGS):
            start = jnp.where(tq >= total, total, start)
            total = total + seg[i]
        return start

    here = z * TB + xlo * TH
    lane = lax.broadcasted_iota(jnp.int32, (TH, HD), 1)
    tok = here + lax.broadcasted_iota(jnp.int32, (TH, HD), 0)
    pos = (tok - firsts(tok)).astype(F32)
    freq = jnp.exp((lax.rem(lane, HALF)).astype(F32) * (-2.0 / HD * math.log(ROPE_BASE)))
    angle = pos * freq
    cosine = jnp.cos(angle)
    sine = jnp.sin(angle)
    sine = jnp.where(lane < HALF, -sine, sine)

    def rotated(v):
        return v * cosine + pltpu.roll(v, HALF, 1) * sine

    x_copy(z).wait_recv()
    fx = []
    totals = []
    for r in range(2):
        rows = slice(r * RS, r * RS + RS)
        z_copy(0, 7, r).wait_recv()
        z_copy(1, 6, r).wait_recv()
        t = own_rows(z, r) + zr[0, 7, rows, :].astype(F32) + zr[1, 6, rows, :].astype(F32)
        totals.append(t[:, 0:XF])
        fx.append(jnp.where(mine_top, t[:, XF : XF + ZF], t[:, XF + ZF : MSG]))
        fxs[rows, :] = jnp.where(mine_top, t[:, XF + ZF : MSG], t[:, XF : XF + ZF]).astype(BF)
    q_copy(0, 7).wait_recv()
    q_copy(1, 6).wait_recv()
    sqx[0] = sq[z] + sqr[0, 7] + sqr[1, 6]
    cp_sq = rc(sqx.at[0], sqx.at[1], f_s.at[0], f_r.at[0], dev_x)
    cp_fx = rc(fxs, fxr, f_s.at[1], f_r.at[1], dev_x)
    go(cp_sq)
    go(cp_fx)
    xsum = jnp.concatenate(totals, axis=0)
    zsum = jnp.concatenate(fx, axis=0)
    cp_sq.wait_recv()
    squares = jnp.transpose(jnp.broadcast_to((sqx[0] + sqx[1])[0:1], (HD, TB)))
    squares = jnp.where(mine_top, squares[0:TH], squares[TH:TB])
    scale = lax.rsqrt(squares / MODEL + EPS)

    def k_slot(d, xx, cc):
        return kvw.at[cc, d, xx]

    def k_copy(d, xx, cc, ss, dev, dd=None):
        return rc(k_slot(d, xx, cc), k_slot(d if dd is None else dd, xx, cc), ss, k_r.at[d if dd is None else dd, xx, cc], dev)

    kv = xsum[:, 0:HD] * scale
    kvw[core, 0, xlo] = jnp.where(is_core0, rotated(kv), kv).astype(BF)
    for d in range(1, WIN):
        go(k_copy(0, xlo, core, kz_s.at[d - 1], at_z(d), d))
    go(k_copy(0, xlo, core, kx_s.at[0], dev_x))
    go(k_copy(0, xlo, core, kc_s.at[0, xlo], dev_c))

    cp_fx.wait_recv()
    zsum = zsum + fxr[...].astype(F32)
    queries = [xsum[:, HD * (1 + j) : HD * (2 + j)] for j in range(2)] + [zsum[:, HD * j : HD * (j + 1)] for j in range(2)]
    queries = jnp.concatenate([rotated(q * scale).astype(BF) for q in queries], axis=0)

    for d in range(WIN):
        if d:
            k_copy(d, xlo, core, kx_s.at[d], dev_x).wait_recv()
            go(k_copy(d, xlo, core, kx_s.at[d], dev_x))
            go(k_copy(d, xlo, core, kc_s.at[d, xlo], dev_c))
        k_copy(d, xot, core, kx_s.at[d], dev_x).wait_recv()
        go(k_copy(d, xot, core, kc_s.at[d, xot], dev_c))
    for d in range(WIN):
        for xx in range(2):
            k_copy(d, xx, cot, kx_s.at[d], dev_c).wait_recv()

    keys = kvw[0].reshape(KEYS, HD)
    values = kvw[1].reshape(KEYS, HD)
    scores = lax.dot_general(queries, keys, nt, preferred_element_type=F32) * (1.0 / math.sqrt(HD))
    n = lax.broadcasted_iota(jnp.int32, (TH, KEYS), 1)
    tk = z * TB + n - 2 * TB * lax.div(n, TB)
    tq = here + lax.broadcasted_iota(jnp.int32, (TH, KEYS), 0)
    allowed = (tk >= firsts(tq)) & (tk <= tq)
    for j in range(4):
        sc = jnp.where(allowed, scores[TH * j : TH * (j + 1)], -1e30)
        e = jnp.exp(sc - jnp.max(sc, axis=1, keepdims=True))
        e = jnp.where(allowed, e, 0.0)
        o = jnp.dot(e.astype(BF), values, preferred_element_type=F32) / jnp.sum(e, axis=1, keepdims=True)
        ref = af if j < 2 else al
        ref[z, xlo, :, HD * (j % 2) : HD * (j % 2 + 1)] = o.astype(BF)

    def unit(u, b):
        return af.at[b, u] if u < 2 else al.at[b, xlo]

    def d_copy(d, u, k, b):
        return rc(unit(u, b), unit(u, b), dz_s.at[d, u, k], d_r.at[u, b], at_z(1 - 2 * d))

    def l_copy(b, xx):
        return rc(al.at[b, xx], al.at[b, xx], dx_s.at[b], d_r.at[3, b], dev_x)

    cp_f = rc(af.at[z, xlo], af.at[z, xlo], dx_s.at[NZ], d_r.at[xlo, z], dev_x)
    cp_f.start()
    l_copy(z, xlo).start()
    for d in range(2):
        rc(af.at[z, xlo], af.at[z, xlo], dz_s.at[d, xlo, 0], d_r.at[xlo, z], at_z(1 - 2 * d)).start()
        d_copy(d, 2, 0, z).start()
    rc(af.at[z, xot], af.at[z, xot], dx_s.at[NZ], d_r.at[xot, z], dev_x).wait_recv()
    for d in range(2):
        rc(af.at[z, xot], af.at[z, xot], dz_s.at[d, xot, 0], d_r.at[xot, z], at_z(1 - 2 * d)).start()

    def pass_on(d, k, b, last):
        for u in range(3):
            d_copy(d, u, k, b).wait_recv()

            @pl.when(k < last)
            def _():
                d_copy(d, u, k, b).start()

        l_copy(b, xlo).start()

    def c_copy(b):
        m = lax.div(b, 2)
        return rc(cs.at[m], cr.at[m], c_s.at[m], c_r.at[m], dev_c)

    def e_copy(b, yy, src_y):
        hh = lax.div(b, 8)
        return rc(es.at[lax.div(b, 2)], er.at[hh, src_y], e_s.at[lax.div(b, 2)], e_r.at[hh, src_y], at_y(yy))

    def out_product(b):
        l_copy(b, xot).wait_recv()
        p = jnp.dot(af[b].reshape(TB, QF), wov[0:QF], preferred_element_type=F32)
        p = p + jnp.dot(al[b].reshape(TB, ZF), wov[QF:], preferred_element_type=F32)

        @pl.when(lax.rem(b, 2) == core)
        def _():
            own[lax.div(b, 2)] = p

        @pl.when(lax.rem(b, 2) != core)
        def _():
            cs[lax.div(b, 2)] = p.astype(BF)
            c_copy(b).start()

    def out_send(b):
        @pl.when(lax.rem(b, 2) == core)
        def _():
            c_copy(b).wait_recv()
            t = own[lax.div(b, 2)] + cr[lax.div(b, 2)].astype(F32)
            yb = lax.rem(lax.div(b, 2), 4)

            @pl.when(yb == y)
            def _():
                el[lax.div(b, 8)] = t

            @pl.when(yb != y)
            def _():
                es[lax.div(b, 2)] = t.astype(BF)
                e_copy(b, yb, y).start()

    def gather_step(k, _):
        pass_on(0, k, zm(z - k), 8)

        @pl.when(k < 8)
        def _():
            pass_on(1, k, zm(z + k), 7)

        out_product(zm(z - k + 1))

        @pl.when(k > 1)
        def _():
            out_product(zm(z + k - 1))
            out_send(zm(z - k + 2))

        @pl.when(k > 2)
        def _():
            out_send(zm(z + k - 2))

        return 0

    lax.fori_loop(1, 9, gather_step, 0)
    out_product(zm(z - 8))
    out_send(zm(z - 7))
    out_send(zm(z + 7))
    out_send(zm(z - 8))

    def y_sum(hh):
        t = el[hh]
        for d in range(1, 4):
            yy = ym(y + d)
            rc(es.at[0], er.at[hh, yy], e_s.at[0], e_r.at[hh, yy], at_y(yy)).wait_recv()
            t = t + er[hh, yy].astype(F32)
        return t

    ex[0] = y_sum(hot).astype(BF)
    cp_e = rc(ex.at[0], ex.at[1], ex_s, ex_r, dev_h)
    cp_e.start()
    mine = y_sum(xhi)
    cp_e.wait_recv()
    out[...] = (mine + ex[1].astype(F32)).astype(BF)

    for c in sends:
        c.wait_send()
    cp_e.wait_send()
    cp_f.wait_send()

    def left(b, _):
        x_copy(b).wait_send()
        l_copy(b, xlo).wait_send()
        return 0

    lax.fori_loop(0, NZ, left, 0)

    def left_z(k, _):
        for d in range(2):

            @pl.when(k < 8 - d)
            def _():
                for r in range(2):
                    z_copy(d, k, r).wait_send()
                q_copy(d, k).wait_send()
                for u in range(3):
                    d_copy(d, u, k, z).wait_send()

        b = 2 * k + cot
        c_copy(b).wait_send()

        @pl.when(lax.rem(k, 4) != y)
        def _():
            e_copy(2 * k, lax.rem(k, 4), y).wait_send()

        return 0

    lax.fori_loop(0, 8, left_z, 0)


def shards(hidden_in, norm_gain, w_query, w_key, w_value, w_out, seg_lengths):
    v = pltpu.VMEM
    dma = pltpu.SemaphoreType.DMA
    scratch = [
        v((NZ, TB, WIDTH), BF),
        v((WIDTH, WIDTH), BF),
        v((2, WIDTH, HD), BF),
        v((WIDTH, WIDTH + HD), BF),
        v((WIDTH, WIDTH), BF),
        v((1, WIDTH), F32),
        v((NZ, TH, MSG), BF),
        v((NZ, TH, XF), BF),
        v((NZ, TH, XF), BF),
        v((2, 8, TH, MSG), BF),
        v((2, 8, TH, MSG), BF),
        v((NZ, 8, TB), F32),
        v((2, 8, 8, TB), F32),
        v((2, 8, 8, TB), F32),
        v((2, 8, TB), F32),
        v((TH, ZF), BF),
        v((TH, ZF), BF),
        v((2, WIN, 2, TH, HD), BF),
        v((NZ, 2, TH, QF), BF),
        v((NZ, 2, TH, ZF), BF),
        v((8, TB, WIDTH), BF),
        v((8, TB, WIDTH), BF),
        v((8, TB, WIDTH), F32),
        v((8, TB, WIDTH), BF),
        v((2, 4, TB, WIDTH), BF),
        v((2, TB, WIDTH), F32),
        v((2, TB, WIDTH), BF),
        dma((6,)),
        dma((15,)), dma((NZ,)),
        dma((NZ,)), dma((NZ,)),
        dma((2, 8, 2)), dma((2, 8, 2)),
        dma((2, 8)), dma((2, 8)),
        dma((2,)), dma((2,)),
        dma((4,)), dma((WIN,)), dma((WIN, 2)), dma((WIN, 2, 2)),
        dma((2, 3, 8)), dma((NZ + 1,)), dma((4, NZ)),
        dma((8,)), dma((8,)),
        dma((8,)), dma((2, 4)),
        dma, dma,
    ]
    anywhere = pl.BlockSpec(memory_space=pl.ANY)
    return pl.pallas_call(
        body,
        name="attention_block",
        out_shape=jax.ShapeDtypeStruct((TB, WIDTH), BF),
        in_specs=[anywhere] * 6 + [pl.BlockSpec(memory_space=pltpu.SMEM)],
        out_specs=pl.BlockSpec(memory_space=pltpu.VMEM),
        scratch_shapes=scratch,
        compiler_params=pltpu.CompilerParams(collective_id=0, has_side_effects=True, vmem_limit_bytes=48 * 2**20),
        cost_estimate=pl.CostEstimate(flops=3 * 10**9, bytes_accessed=3 * 10**6, transcendentals=10**6),
    )(hidden_in, norm_gain.reshape(1, WIDTH), w_query, w_key, w_value, w_out, seg_lengths)


def solution(mesh):
    in_specs = (P("gy", "gx"), P("gx"), P("gx", "gy"), P("gx", None), P("gx", None), P("gy", "gx"), P())
    return jax.shard_map(shards, mesh=mesh, in_specs=in_specs, out_specs=P("gy", "gx"), check_vma=False)
```

time: 758 us -> 136 us (0.18)
  the two profiles are of different devices: /device:TPU:1 before, /device:TPU:38 now
where the time goes in v1:
time: 136 us
  Pallas kernels  128 us (94%)
  local copies, waits for them, and re-layouts  7.43 us (5%)
    pallas_call x1, Pallas kernels, shards(): pl.pallas_call(body, name='attention_block', out_shape=jax.ShapeDtypeStru...  128 us
    unnamed x15, local copies, waits for them, and re-layouts  7.43 us

profile of v1, /device:TPU:38, one launch (start us, length us, event | category | flops | bytes accessed | tf_op | source)
XLA Modules:
  0.0 135.8 jit_solution(1905056233030596935)
XLA Ops:
  0.0 0.0 copy-start.6
  0.0 0.7 copy-done.6
  0.7 0.0 copy-start
  0.7 1.2 copy-done
  1.9 0.0 copy-start.1
  1.9 1.2 copy-done.1
  3.1 0.0 copy-start.2
  3.1 1.0 copy-done.2
  4.1 0.0 copy-start.3
  4.2 1.0 copy-done.3
  5.2 0.0 copy-start.4
  5.2 0.9 copy-done.4
  6.1 0.0 copy-start.5
  6.1 0.7 copy-done.5
  6.8 128.4 %attention_block.1 = bf16[128,512]{1,0:T(8,128)(2,1)S(1)} custom-call(bf16[128,512]{1,0:T(8,128)(2,1)S(1)} %copy-done.4, f32[1,512]{1,0:T(1,128)S(1)} %bitcast.1, bf16[512,512]{1,0:T(8,128)(2,1)S(1)} %copy-done.2, bf16[512,1024]{1,0:T(8,128)(2,1)S(1)} %copy-done, bf16[512,1024]{1,0:T(8,128)(2,1)S(1)} %copy-done.1, bf16[512,512]{1,0:T(8,128)(2,1)S(1)} %copy-done.3, ...), custom_call_target="tpu_custom_call" | custom-call | flops 3000000000 | bytes 3000000 | tf_op jit(solution)/shard_map/attention_block/pallas_call | solution.py:476
  135.1 0.7 copy.9
Async XLA Ops:
  0.0 0.7 copy-start.6
  0.7 1.2 copy-start
  1.9 1.2 copy-start.1
  3.1 1.0 copy-start.2
  4.1 1.0 copy-start.3
  5.2 0.9 copy-start.4
  6.1 0.7 copy-start.5

commit v2 on v0

v2 whole, which is shorter than its diff:
```python
import math

import jax
import jax.numpy as jnp
from jax import lax
from jax.experimental import pallas as pl
from jax.experimental.pallas import tpu as pltpu
from jax.sharding import PartitionSpec as P

MESH = pl.DeviceIdType.MESH
HD = 128
HALF = HD // 2
SEGS = 8
ROPE_BASE = 500000.0
EPS = 1e-05
BF = jnp.bfloat16
F32 = jnp.float32

NZ = 16
TB = 128
TH = 64
WIDTH = 512
QW = 256
COLS = HD + WIDTH
WIN = 5
KEYS = WIN * TB
MODEL = 16384


def body(h, gain, wq, wk, wv, wo, seg, out, *s):
    (
        gath, wraw, kvraw, wcat, wov, gv, segs, part, zk, zkr, zq, zqr, sq, sqs, sqr, kvw, att, cs, cr, own, es, er, el, xs, xr,
        in_sem, ga_s, ga_r, gc_r, w_s, w_r, zk_s, zk_r, zq_s, zq_r, q_s, q_r, k_s, k_r, kc_r, d_s, d_r, c_s, c_r, e_s, e_r, x_s, x_r,
    ) = s
    gx = lax.axis_index("gx")
    gy = lax.axis_index("gy")
    xlo, z = lax.div(gx, NZ), lax.rem(gx, NZ)
    xhi, y, core = lax.div(gy, 8), lax.rem(lax.div(gy, 2), 4), lax.rem(gy, 2)
    xot, hot, cot = 1 - xlo, 1 - xhi, 1 - core

    def zm(v):
        return lax.rem(v + NZ, NZ)

    def ym(v):
        return lax.rem(v + 4, 4)

    def at_z(d):
        return {"gx": xlo * NZ + zm(z + d), "gy": gy}

    def at_y(yy):
        return {"gx": gx, "gy": xhi * 8 + yy * 2 + core}

    def blk(hh, yy, cc):
        return hh * 8 + yy * 2 + cc

    far = blk(hot, y, core)
    dev_x = {"gx": xot * NZ + z, "gy": gy}
    dev_h = {"gx": gx, "gy": far}
    dev_d = {"gx": xot * NZ + z, "gy": far}
    dev_c = {"gx": gx, "gy": blk(xhi, y, cot)}

    def rc(src, dst, ss, rs, dev):
        return pltpu.make_async_remote_copy(src_ref=src, dst_ref=dst, send_sem=ss, recv_sem=rs, device_id=dev, device_id_type=MESH)

    barrier = pltpu.get_barrier_semaphore()
    greet = [dev_x, dev_h, dev_d, dev_c] + [at_y(ym(y + d)) for d in (1, 2, 3)] + [at_z(d) for d in (1, 2, 3, 4, -1, -2, -3, -4)]
    for d in greet:
        pl.semaphore_signal(barrier, inc=1, device_id=d, device_id_type=MESH)
    is_core0 = core == 0
    head = pl.multiple_of((xhi * 4 + y) * HD, HD)
    mine = pl.ds(pl.multiple_of(xlo * TH, TH), TH)
    other = pl.ds(pl.multiple_of(xot * TH, TH), TH)
    loads = [
        pltpu.make_async_copy(h.at[mine], gath.at[gy, 0], in_sem.at[0]),
        pltpu.make_async_copy(wq, wraw.at[0], in_sem.at[1]),
        pltpu.make_async_copy(wo, wov.at[0], in_sem.at[2]),
        pltpu.make_async_copy(gain, gv.at[0], in_sem.at[3]),
        pltpu.make_async_copy(seg, segs, in_sem.at[4]),
    ]
    for c in loads:
        c.start()

    def kv_load(src):
        return pltpu.make_async_copy(src.at[:, pl.ds(head, HD)], kvraw.at[0], in_sem.at[5])

    def kv_send(src):
        return rc(src.at[:, pl.ds(head, HD)], kvraw.at[1], w_s.at[0], w_r.at[0], dev_x)

    @pl.when(is_core0)
    def _():
        kv_load(wk).start()

    @pl.when(core == 1)
    def _():
        kv_load(wv).start()

    pl.semaphore_wait(barrier, len(greet))

    def g_copy(dst, n, dev, src=None):
        return rc(dst if src is None else src, dst, ga_s, ga_r.at[n], dev)

    def gc_copy(ref):
        return rc(ref, ref, ga_s, gc_r, dev_c)

    ys = (1, 3, 2)
    at = {1: 4, 3: 1, 2: 7}
    by = {1: 1, 3: 4, 2: 7}
    g_copy(gath.at[gy, 1], 0, dev_x, h.at[other]).start()
    g_copy(gath.at[gy, 0], 10, dev_h, h.at[mine]).start()
    g_copy(gath.at[gy, 1], 11, dev_d, h.at[other]).start()
    for d in ys:
        g_copy(gath.at[gy, 0], at[d], at_y(ym(y + d)), h.at[mine]).start()

    @pl.when(is_core0)
    def _():
        kv_send(wk).start()

    @pl.when(core == 1)
    def _():
        kv_send(wv).start()

    cp_g = rc(gain, gv.at[1], w_s.at[1], w_r.at[1], dev_x)
    cp_q = rc(wq, wraw.at[1], w_s.at[2], w_r.at[2], dev_x)
    cp_o = rc(wo, wov.at[1], w_s.at[3], w_r.at[3], dev_x)
    cp_g.start()
    cp_q.start()
    rc(h.at[mine], gath.at[gy, 0], ga_s, gc_r, dev_c).start()

    for c in loads:
        c.wait()
    kv_load(wk).wait()

    def weights(f):
        col = jnp.transpose(jnp.broadcast_to(gv[f], (HD, WIDTH)))
        wcat[f, :, 0:HD] = (kvraw[f].astype(F32) * col).astype(BF)
        for j in range(WIDTH // HD):
            wcat[f, :, HD * (j + 1) : HD * (j + 2)] = (wraw[f, :, HD * j : HD * (j + 1)].astype(F32) * col).astype(BF)

    g_copy(gath.at[gy, 1], 0, dev_x).wait_recv()
    for d in ys:
        g_copy(gath.at[gy, 1], at[d] + 1, at_y(ym(y + d))).start()
    gc_copy(gath.at[gy, 1]).start()
    g_copy(gath.at[far, 0], 10, dev_h).wait_recv()
    g_copy(gath.at[far, 1], 11, dev_d).wait_recv()
    for d in ys:
        g_copy(gath.at[far], at[d] + 2, at_y(ym(y + d))).start()
    gc_copy(gath.at[far]).start()
    weights(0)

    def firsts(tq):
        start = jnp.zeros_like(tq)
        total = jnp.int32(0)
        for i in range(SEGS):
            start = jnp.where(tq >= total, total, start)
            total = total + segs[i]
        return start

    here = z * TB + xlo * TH
    lane = lax.broadcasted_iota(jnp.int32, (TH, HD), 1)
    tok = here + lax.broadcasted_iota(jnp.int32, (TH, HD), 0)
    pos = (tok - firsts(tok)).astype(F32)
    freq = jnp.exp((lax.rem(lane, HALF)).astype(F32) * (-2.0 / HD * math.log(ROPE_BASE)))
    angle = pos * freq
    cosine = jnp.cos(angle)
    sine = jnp.sin(angle)
    sine = jnp.where(lane < HALF, -sine, sine)

    def rotated(v):
        return v * cosine + pltpu.roll(v, HALF, 1) * sine

    for d in ys:
        b = blk(xhi, ym(y + d), core)
        g_copy(gath.at[b, 0], by[d], dev_c).wait_recv()
        g_copy(gath.at[b, 1], by[d] + 1, dev_c).wait_recv()
        gc_copy(gath.at[b]).start()
    for d in ys:
        b = blk(hot, ym(y + d), core)
        g_copy(gath.at[b], by[d] + 2, dev_c).wait_recv()
        gc_copy(gath.at[b]).start()
    rc(kvraw.at[0], kvraw.at[1], w_s.at[0], w_r.at[0], dev_x).wait_recv()
    cp_g.wait_recv()
    cp_q.wait_recv()
    cp_o.start()
    weights(1)
    gc_copy(gath.at[pl.ds(0, 8)]).wait_recv()

    ones = jnp.ones((8, WIDTH), BF)
    nt = (((1,), (1,)), ((), ()))

    def product(i):
        bp, bm = zm(z + 8 - i), zm(z - 7 + i)
        res = jnp.zeros((TB, COLS), F32)
        sums = jnp.zeros((8, TB), F32)
        for f in range(2):
            x = jnp.concatenate([gath[bp, f], gath[bm, f]], axis=0)
            res = res + jnp.dot(x, wcat[f], preferred_element_type=F32)
            xf = x.astype(F32)
            x2 = xf * xf
            hi = x2.astype(BF)
            lo = (x2 - hi.astype(F32)).astype(BF)
            sums = sums + lax.dot_general(ones, hi, nt, preferred_element_type=F32) + lax.dot_general(ones, lo, nt, preferred_element_type=F32)
        part[i] = res
        sq[i, 0] = sums
        sq[i, 1] = pltpu.roll(sums, TH, 1)

    def k_ring(d, k):
        return rc(zk.at[d, k], zkr.at[d, k], zk_s.at[d], zk_r.at[d, k], at_z(1 - 2 * d))

    def q_ring(d, k, p):
        return rc(zq.at[d, k, p], zqr.at[d, k, p], zq_s.at[d], zq_r.at[d, k, p], at_z(1 - 2 * d))

    def s_ring(d, k):
        return rc(sqs.at[d, k], sqr.at[d, k], q_s.at[d], q_r.at[d, k], at_z(1 - 2 * d))

    def mix(k, first, later):
        @pl.when(k == 0)
        def _():
            first()

        @pl.when(k > 0)
        def _():
            later()

    def send_kv(d, k):
        rows = slice(d * TH, d * TH + TH)

        def first():
            zk[d, k] = part[k, rows, 0:HD].astype(BF)

        def later():
            k_ring(d, k - 1).wait_recv()
            zk[d, k] = (part[k, rows, 0:HD] + zkr[d, k - 1].astype(F32)).astype(BF)

        mix(k, first, later)
        k_ring(d, k).start()

    def send_q(d, k, p):
        rows = slice(d * TH, d * TH + TH)
        cols = slice(HD + p * QW, HD + p * QW + QW)

        def first():
            zq[d, k, p] = part[k, rows, cols].astype(BF)

        def later():
            q_ring(d, k - 1, p).wait_recv()
            zq[d, k, p] = (part[k, rows, cols] + zqr[d, k - 1, p].astype(F32)).astype(BF)

        mix(k, first, later)
        q_ring(d, k, p).start()

    def send_sq(d, k):
        def first():
            sqs[d, k] = sq[k, d]

        def later():
            s_ring(d, k - 1).wait_recv()
            sqs[d, k] = sq[k, d] + sqr[d, k - 1]

        mix(k, first, later)
        s_ring(d, k).start()

    def ring_dir(d, k):
        send_kv(d, k)
        for p in range(2):
            send_q(d, k, p)
        send_sq(d, k)

    product(0)

    def reduce_step(k, _):
        ring_dir(0, k)

        @pl.when(k < 7)
        def _():
            ring_dir(1, k)
            product(k + 1)

        return 0

    lax.fori_loop(0, 8, reduce_step, 0)

    s_ring(0, 7).wait_recv()
    s_ring(1, 6).wait_recv()
    squares = (sq[7, 1] + sqr[0, 7] + sqr[1, 6])[0:1]
    squares = jnp.transpose(jnp.broadcast_to(squares, (HD, TB)))[0:TH]
    scale = lax.rsqrt(squares / MODEL + EPS)

    def k_copy(d, xx, n, dev, dd=None):
        to = d if dd is None else dd
        return rc(kvw.at[core, d, xx], kvw.at[core, to, xx], k_s, k_r.at[to, n], dev)

    def kc_copy(d, xx):
        return rc(kvw.at[core, d, xx], kvw.at[core, d, xx], k_s, kc_r, dev_c)

    k_ring(0, 7).wait_recv()
    k_ring(1, 6).wait_recv()
    kv = (part[7, TH:TB, 0:HD] + zkr[0, 7].astype(F32) + zkr[1, 6].astype(F32)) * scale
    kvw[core, 0, xlo] = jnp.where(is_core0, rotated(kv), kv).astype(BF)
    for d in range(WIN - 1, 0, -1):
        k_copy(0, xlo, 0, at_z(d), d).start()
    k_copy(0, xlo, 1, dev_x).start()
    kc_copy(0, xlo).start()

    queries = []
    for p in range(2):
        q_ring(0, 7, p).wait_recv()
        q_ring(1, 6, p).wait_recv()
        t = part[7, TH:TB, HD + p * QW : HD + p * QW + QW] + zqr[0, 7, p].astype(F32) + zqr[1, 6, p].astype(F32)
        for j in range(2):
            queries.append(rotated(t[:, HD * j : HD * (j + 1)] * scale).astype(BF))
    queries = jnp.concatenate(queries, axis=0)

    for d in range(1, WIN):
        k_copy(d, xlo, 0, dev_x).wait_recv()
        k_copy(d, xlo, 1, dev_x).start()
        kc_copy(d, xlo).start()
    for d in range(WIN):
        k_copy(d, xot, 1, dev_x).wait_recv()
        kc_copy(d, xot).start()
    rc(kvw.at[cot], kvw.at[cot], k_s, kc_r, dev_c).wait_recv()

    keys = kvw[0].reshape(KEYS, HD)
    values = kvw[1].reshape(KEYS, HD)
    scores = lax.dot_general(queries, keys, nt, preferred_element_type=F32) * (1.0 / math.sqrt(HD))
    n = lax.broadcasted_iota(jnp.int32, (TH, KEYS), 1)
    tk = z * TB + n - 2 * TB * lax.div(n, TB)
    tq = here + lax.broadcasted_iota(jnp.int32, (TH, KEYS), 0)
    allowed = (tk >= firsts(tq)) & (tk <= tq)

    def d_copy(d, b, p):
        return rc(att.at[b, p], att.at[b, p], d_s.at[d], d_r.at[b, p], at_z(1 - 2 * d))

    for j in range(4):
        sc = jnp.where(allowed, scores[TH * j : TH * (j + 1)], -1e30)
        e = jnp.exp(sc - jnp.max(sc, axis=1, keepdims=True))
        e = jnp.where(allowed, e, 0.0)
        o = jnp.dot(e.astype(BF), values, preferred_element_type=F32) / jnp.sum(e, axis=1, keepdims=True)
        att[z, j // 2, :, HD * (j % 2) : HD * (j % 2 + 1)] = o.astype(BF)
        if j % 2:
            for d in range(2):
                d_copy(d, z, j // 2).start()
    cp_o.wait_recv()

    def pass_on(d, k, b, last):
        for p in range(2):
            d_copy(d, b, p).wait_recv()

            @pl.when(k < last)
            def _():
                d_copy(d, b, p).start()

    def c_copy(b):
        m = lax.div(b, 2)
        return rc(cs.at[m], cr.at[m], c_s, c_r.at[m], dev_c)

    def e_copy(b, yy):
        hh, m = lax.div(b, 8), lax.div(b, 2)
        return rc(es.at[m], er.at[hh, y], e_s, e_r.at[hh, y], at_y(yy))

    def out_product(blocks):
        halves = [jnp.concatenate([att[b, p] for b in blocks], axis=0) for p in range(2)]
        for g in range(2):
            t = sum(jnp.dot(halves[p], wov[g, p * QW : p * QW + QW], preferred_element_type=F32) for p in range(2))
            cols = slice(g * WIDTH, g * WIDTH + WIDTH)
            same = lax.rem(blocks[0], 2) == core

            @pl.when(same)
            def _():
                for i, b in enumerate(blocks):
                    own[lax.div(b, 2), :, cols] = t[i * TH : i * TH + TH]

            @pl.when(jnp.logical_not(same))
            def _():
                for i, b in enumerate(blocks):
                    cs[lax.div(b, 2), :, cols] = t[i * TH : i * TH + TH].astype(BF)

        @pl.when(lax.rem(blocks[0], 2) != core)
        def _():
            for b in blocks:
                c_copy(b).start()

    def out_send(b):
        @pl.when(lax.rem(b, 2) == core)
        def _():
            m = lax.div(b, 2)
            c_copy(b).wait_recv()
            t = own[m] + cr[m].astype(F32)
            yb = lax.rem(m, 4)

            @pl.when(yb == y)
            def _():
                el[lax.div(b, 8)] = t

            @pl.when(yb != y)
            def _():
                es[m] = t.astype(BF)
                e_copy(b, yb).start()

    def gather_step(k, _):
        pass_on(0, k, zm(z - k), 8)

        @pl.when(k < 8)
        def _():
            pass_on(1, k, zm(z + k), 7)

        @pl.when(k == 1)
        def _():
            out_product([z])

        @pl.when(k > 1)
        def _():
            out_product([zm(z - k + 1), zm(z + k - 1)])
            out_send(zm(z - k + 2))

        @pl.when(k > 2)
        def _():
            out_send(zm(z + k - 2))

        return 0

    lax.fori_loop(1, 9, gather_step, 0)
    out_product([zm(z - 8)])
    out_send(zm(z - 7))
    out_send(zm(z + 7))
    out_send(zm(z - 8))

    def y_sum(hh):
        t = el[hh]
        for d in ys:
            yy = ym(y + d)
            rc(es.at[0], er.at[hh, yy], e_s, e_r.at[hh, yy], at_y(yy)).wait_recv()
            t = t + er[hh, yy].astype(F32)
        return t

    def x_copy(n, dev):
        return rc(xs.at[n], xr.at[n], x_s, x_r.at[n], dev)

    away = y_sum(hot)
    xs[0] = away[:, 0:WIDTH].astype(BF)
    x_copy(0, dev_h).start()
    xs[1] = away[:, WIDTH:].astype(BF)
    x_copy(1, dev_d).start()
    home = y_sum(xhi)
    xs[2] = home[:, WIDTH:].astype(BF)
    x_copy(2, dev_x).start()
    x_copy(0, dev_h).wait_recv()
    out[mine, :] = (home[:, 0:WIDTH] + xr[0].astype(F32)).astype(BF)
    x_copy(1, dev_d).wait_recv()
    x_copy(2, dev_x).wait_recv()
    out[other, :] = (xr[1].astype(F32) + xr[2].astype(F32)).astype(BF)

    def left(ref, sem):
        rc(ref, ref, sem, x_r.at[0], dev_x).wait_send()

    pieces = gath.reshape(2 * NZ, TH, WIDTH)
    left(pieces.at[pl.ds(0, 31)], ga_s)
    left(kvraw.at[0], w_s.at[0])
    cp_g.wait_send()
    cp_q.wait_send()
    cp_o.wait_send()
    for d in range(2):
        left(zk.at[d, pl.ds(0, 8 - d)], zk_s.at[d])
        left(zq.at[d, pl.ds(0, 8 - d)], zq_s.at[d])
        left(sqs.at[d, pl.ds(0, 8 - d)], q_s.at[d])
        left(att.at[pl.ds(0, 8 - d)], d_s.at[d])
    left(kvw.reshape(4 * WIN, TH, HD).at[pl.ds(0, 4 * WIN - 1)], k_s)
    left(cs, c_s)
    left(es.at[pl.ds(0, 6)], e_s)
    left(xs, x_s)


def shards(hidden_in, norm_gain, w_query, w_key, w_value, w_out, seg_lengths):
    v = pltpu.VMEM
    dma = pltpu.SemaphoreType.DMA
    scratch = [
        v((NZ, 2, TH, WIDTH), BF),
        v((2, WIDTH, WIDTH), BF),
        v((2, WIDTH, HD), BF),
        v((2, WIDTH, COLS), BF),
        v((2, WIDTH, WIDTH), BF),
        v((2, 1, WIDTH), F32),
        pltpu.SMEM((SEGS,), jnp.int32),
        v((8, TB, COLS), F32),
        v((2, 8, TH, HD), BF),
        v((2, 8, TH, HD), BF),
        v((2, 8, 2, TH, QW), BF),
        v((2, 8, 2, TH, QW), BF),
        v((8, 2, 8, TB), F32),
        v((2, 8, 8, TB), F32),
        v((2, 8, 8, TB), F32),
        v((2, WIN, 2, TH, HD), BF),
        v((NZ, 2, TH, QW), BF),
        v((8, TH, 2 * WIDTH), BF),
        v((8, TH, 2 * WIDTH), BF),
        v((8, TH, 2 * WIDTH), F32),
        v((8, TH, 2 * WIDTH), BF),
        v((2, 4, TH, 2 * WIDTH), BF),
        v((2, TH, 2 * WIDTH), F32),
        v((3, TH, WIDTH), BF),
        v((3, TH, WIDTH), BF),
        dma((6,)),
        dma, dma((12,)), dma,
        dma((4,)), dma((4,)),
        dma((2,)), dma((2, 8)),
        dma((2,)), dma((2, 8, 2)),
        dma((2,)), dma((2, 8)),
        dma, dma((WIN, 2)), dma,
        dma((2,)), dma((NZ, 2)),
        dma, dma((8,)),
        dma, dma((2, 4)),
        dma, dma((3,)),
    ]
    anywhere = pl.BlockSpec(memory_space=pl.ANY)
    return pl.pallas_call(
        body,
        name="attention_block",
        out_shape=jax.ShapeDtypeStruct((TB, WIDTH), BF),
        in_specs=[anywhere] * 7,
        out_specs=pl.BlockSpec(memory_space=pltpu.VMEM),
        scratch_shapes=scratch,
        compiler_params=pltpu.CompilerParams(collective_id=0, has_side_effects=True, vmem_limit_bytes=62 * 2**20),
        cost_estimate=pl.CostEstimate(flops=3 * 10**9, bytes_accessed=3 * 10**6, transcendentals=10**6),
    )(hidden_in, norm_gain.reshape(1, WIDTH), w_query, w_key, w_value, w_out, seg_lengths)


def solution(mesh):
    in_specs = (P("gy", "gx"), P("gx"), P("gx", "gy"), P("gx", None), P("gx", None), P("gy", "gx"), P())
    return jax.shard_map(shards, mesh=mesh, in_specs=in_specs, out_specs=P("gy", "gx"), check_vma=False)
```

time: 758 us -> 115 us (0.15)
  waiting for transfers between devices: 662 us -> 0 us
  Pallas kernels: 0 us -> 113 us
  blocking collectives: 57.2 us -> 0 us
  between operations: 13.3 us -> 0.01 us
  matrix products: 13.2 us -> 0 us
  other arithmetic: 8.63 us -> 0 us
    reduce_scatter x2 -> x0, waiting for transfers between devices: 236 us -> none  [the longest x1 129 us: shards(): lax.psum_scatter(jnp.dot(gathered, w_query, preferred_element_type=jnp.fl...]
    psum x1 -> x0, waiting for transfers between devices: 230 us -> none  [shards(): lax.psum(pair_part.astype(jnp.bfloat16), 'gx').astype(jnp.float32)]
    all_gather x2 -> x0, waiting for transfers between devices: 196 us -> none  [the longest x1 128 us: shards(): lax.all_gather(attended, 'gx', axis=0, tiled=True)]
    pallas_call x0 -> x1, Pallas kernels: none -> 113 us  [shards(): pl.pallas_call(body, name='attention_block', out_shape=jax.ShapeDtypeStru...]
    psum x1 -> x0, blocking collectives: 57.2 us -> none  [shards(): squares = lax.psum(jnp.sum(widened * widened, axis=1), 'gx')]
    dot_general x6 -> x0, matrix products: 13.2 us -> none  [the longest x1 4.14 us: shards(): jnp.dot(lax.all_gather(attended, 'gx', axis=0, tiled=True), w_out, prefer...]
  transfers between devices with their start and end apart: 5 -> 0, of which waited for: 5 -> 0; matrix products, arithmetic and copies ran while one was open for 1% -> 0% of each run, Pallas kernels for 0% -> 0%
where the time goes in v2:
time: 115 us
  Pallas kernels  113 us (98%)
  local copies, waits for them, and re-layouts  1.57 us (1%)
    pallas_call x1, Pallas kernels, shards(): pl.pallas_call(body, name='attention_block', out_shape=jax.ShapeDtypeStru...  113 us

profile of v2, /device:TPU:1, one launch (start us, length us, event | category | flops | bytes accessed | tf_op | source)
XLA Modules:
  0.0 114.8 jit_solution(7321451719050348849)
XLA Ops:
  0.0 113.2 %attention_block.1 = bf16[128,512]{1,0:T(8,128)(2,1)} custom-call(bf16[128,512]{1,0:T(8,128)(2,1)} %h.1, f32[1,512]{1,0:T(1,128)} %bitcast.1, bf16[512,512]{1,0:T(8,128)(2,1)} %wq.1, bf16[512,1024]{1,0:T(8,128)(2,1)} %wk.1, bf16[512,1024]{1,0:T(8,128)(2,1)} %wv.1, bf16[512,512]{1,0:T(8,128)(2,1)} %wo.1, s32[8]{0:T(128)} %seg.1), custom_call_target="tpu_custom_call" | custom-call | flops 3000000000 | bytes 3000000 | tf_op jit(solution)/shard_map/attention_block/pallas_call | solution.py:514
  113.2 1.6 %copy.9 = bf16[128,512]{1,0:T(8,128)(2,1)} copy(bf16[128,512]{1,0:T(8,128)(2,1)} %attention_block.1) | data formatting | bytes 262144

commit v3 on v2

--- a/solution.py
+++ b/solution.py
@@ -22,6 +22,8 @@
 WIDTH = 512
 QW = 256
 COLS = HD + WIDTH
+JK = 4
+JQ = 3
 WIN = 5
 KEYS = WIN * TB
 MODEL = 16384
@@ -29,7 +31,7 @@
 
 def body(h, gain, wq, wk, wv, wo, seg, out, *s):
     (
-        gath, wraw, kvraw, wcat, wov, gv, segs, part, zk, zkr, zq, zqr, sq, sqs, sqr, kvw, att, cs, cr, own, es, er, el, xs, xr,
+        gath, wraw, kvraw, wcat, wov, gv, segs, part, kvp, zk, zkr, zq, zqr, sqp, sqs, sqr, kvw, att, cs, cr, own, es, er, el, xs, xr,
         in_sem, ga_s, ga_r, gc_r, w_s, w_r, zk_s, zk_r, zq_s, zq_r, q_s, q_r, k_s, k_r, kc_r, d_s, d_r, c_s, c_r, e_s, e_r, x_s, x_r,
     ) = s
     gx = lax.axis_index("gx")
@@ -111,28 +113,24 @@
     for d in ys:
         g_copy(gath.at[gy, 0], at[d], at_y(ym(y + d)), h.at[mine]).start()
 
-    @pl.when(is_core0)
-    def _():
-        kv_send(wk).start()
-
-    @pl.when(core == 1)
-    def _():
-        kv_send(wv).start()
-
     cp_g = rc(gain, gv.at[1], w_s.at[1], w_r.at[1], dev_x)
     cp_q = rc(wq, wraw.at[1], w_s.at[2], w_r.at[2], dev_x)
     cp_o = rc(wo, wov.at[1], w_s.at[3], w_r.at[3], dev_x)
     cp_g.start()
-    cp_q.start()
     rc(h.at[mine], gath.at[gy, 0], ga_s, gc_r, dev_c).start()
 
     for c in loads:
         c.wait()
     kv_load(wk).wait()
 
-    def weights(f):
-        col = jnp.transpose(jnp.broadcast_to(gv[f], (HD, WIDTH)))
-        wcat[f, :, 0:HD] = (kvraw[f].astype(F32) * col).astype(BF)
+    def gain_column(f):
+        return jnp.transpose(jnp.broadcast_to(gv[f], (HD, WIDTH)))
+
+    def kv_weights(f):
+        wcat[f, :, 0:HD] = (kvraw[f].astype(F32) * gain_column(f)).astype(BF)
+
+    def q_weights(f):
+        col = gain_column(f)
         for j in range(WIDTH // HD):
             wcat[f, :, HD * (j + 1) : HD * (j + 2)] = (wraw[f, :, HD * j : HD * (j + 1)].astype(F32) * col).astype(BF)
 
@@ -145,7 +143,17 @@
     for d in ys:
         g_copy(gath.at[far], at[d] + 2, at_y(ym(y + d))).start()
     gc_copy(gath.at[far]).start()
-    weights(0)
+    @pl.when(is_core0)
+    def _():
+        kv_send(wk).start()
+
+    @pl.when(core == 1)
+    def _():
+        kv_send(wv).start()
+
+    cp_q.start()
+    kv_weights(0)
+    q_weights(0)
 
     def firsts(tq):
         start = jnp.zeros_like(tq)
@@ -179,109 +187,104 @@
         gc_copy(gath.at[b]).start()
     rc(kvraw.at[0], kvraw.at[1], w_s.at[0], w_r.at[0], dev_x).wait_recv()
     cp_g.wait_recv()
-    cp_q.wait_recv()
-    cp_o.start()
-    weights(1)
+    kv_weights(1)
     gc_copy(gath.at[pl.ds(0, 8)]).wait_recv()
 
     ones = jnp.ones((8, WIDTH), BF)
     nt = (((1,), (1,)), ((), ()))
 
-    def product(i):
-        bp, bm = zm(z + 8 - i), zm(z - 7 + i)
-        res = jnp.zeros((TB, COLS), F32)
-        sums = jnp.zeros((8, TB), F32)
+    def steps(j):
+        heads = [(0, 8), (0, j - 1), (1, 7), (1, j - 1)]
+        ends = [j, 1, j, 1]
+        return [[(d, n - t) for (d, n), e in zip(heads, ends) if n - t >= e] for t in range(9 - j)]
+
+    def target(d, n):
+        return zm(z + (1 - 2 * d) * n)
+
+    def leg(d, n, j):
+        return at_z((1 - 2 * d) * (j if n == j else 1))
+
+    def k_ring(d, n):
+        return rc(zk.at[d, n], zkr.at[d, n], zk_s.at[d], zk_r.at[d, n], leg(d, n, JK))
+
+    def q_ring(d, n):
+        return rc(zq.at[d, n], zqr.at[d, n], zq_s.at[d], zq_r.at[d, n], leg(d, n, JQ))
+
+    def s_ring(d, n):
+        return rc(sqs.at[d, n], sqr.at[d, n], q_s.at[d], q_r.at[d, n], leg(d, n, JK))
+
+    def add_on(d, n, j, mine, ring, stage, got):
+        t = mine
+        if n + 1 <= 8 - d and n + 1 != j:
+            ring(d, n + 1).wait_recv()
+            t = t + got[d, n + 1].astype(F32)
+        stage[d, n] = t.astype(stage.dtype)
+        ring(d, n).start()
+
+    def total(j, mine, ring, got):
+        t = mine
+        for d in range(2):
+            for n in (1, j):
+                ring(d, n).wait_recv()
+                t = t + got[d, n].astype(F32)
+        return t
+
+    def rows_of(pairs, f):
+        return jnp.concatenate([gath[target(d, n), f] for d, n in pairs], axis=0)
+
+    def q_product(pairs):
+        res = sum(jnp.dot(rows_of(pairs, f), wcat[f, :, HD:], preferred_element_type=F32) for f in range(2))
+        for i, (d, n) in enumerate(pairs):
+            part[d, n] = res[i * TH : i * TH + TH]
+
+    def sq_product(pairs):
+        r = jnp.zeros((8, len(pairs) * TH), F32)
         for f in range(2):
-            x = jnp.concatenate([gath[bp, f], gath[bm, f]], axis=0)
-            res = res + jnp.dot(x, wcat[f], preferred_element_type=F32)
-            xf = x.astype(F32)
+            xf = rows_of(pairs, f).astype(F32)
             x2 = xf * xf
             hi = x2.astype(BF)
             lo = (x2 - hi.astype(F32)).astype(BF)
-            sums = sums + lax.dot_general(ones, hi, nt, preferred_element_type=F32) + lax.dot_general(ones, lo, nt, preferred_element_type=F32)
-        part[i] = res
-        sq[i, 0] = sums
-        sq[i, 1] = pltpu.roll(sums, TH, 1)
-
-    def k_ring(d, k):
-        return rc(zk.at[d, k], zkr.at[d, k], zk_s.at[d], zk_r.at[d, k], at_z(1 - 2 * d))
-
-    def q_ring(d, k, p):
-        return rc(zq.at[d, k, p], zqr.at[d, k, p], zq_s.at[d], zq_r.at[d, k, p], at_z(1 - 2 * d))
-
-    def s_ring(d, k):
-        return rc(sqs.at[d, k], sqr.at[d, k], q_s.at[d], q_r.at[d, k], at_z(1 - 2 * d))
-
-    def mix(k, first, later):
-        @pl.when(k == 0)
-        def _():
-            first()
-
-        @pl.when(k > 0)
-        def _():
-            later()
-
-    def send_kv(d, k):
-        rows = slice(d * TH, d * TH + TH)
-
-        def first():
-            zk[d, k] = part[k, rows, 0:HD].astype(BF)
-
-        def later():
-            k_ring(d, k - 1).wait_recv()
-            zk[d, k] = (part[k, rows, 0:HD] + zkr[d, k - 1].astype(F32)).astype(BF)
-
-        mix(k, first, later)
-        k_ring(d, k).start()
-
-    def send_q(d, k, p):
-        rows = slice(d * TH, d * TH + TH)
-        cols = slice(HD + p * QW, HD + p * QW + QW)
-
-        def first():
-            zq[d, k, p] = part[k, rows, cols].astype(BF)
-
-        def later():
-            q_ring(d, k - 1, p).wait_recv()
-            zq[d, k, p] = (part[k, rows, cols] + zqr[d, k - 1, p].astype(F32)).astype(BF)
-
-        mix(k, first, later)
-        q_ring(d, k, p).start()
-
-    def send_sq(d, k):
-        def first():
-            sqs[d, k] = sq[k, d]
-
-        def later():
-            s_ring(d, k - 1).wait_recv()
-            sqs[d, k] = sq[k, d] + sqr[d, k - 1]
-
-        mix(k, first, later)
-        s_ring(d, k).start()
-
-    def ring_dir(d, k):
-        send_kv(d, k)
-        for p in range(2):
-            send_q(d, k, p)
-        send_sq(d, k)
-
-    product(0)
-
-    def reduce_step(k, _):
-        ring_dir(0, k)
-
-        @pl.when(k < 7)
-        def _():
-            ring_dir(1, k)
-            product(k + 1)
-
-        return 0
-
-    lax.fori_loop(0, 8, reduce_step, 0)
-
-    s_ring(0, 7).wait_recv()
-    s_ring(1, 6).wait_recv()
-    squares = (sq[7, 1] + sqr[0, 7] + sqr[1, 6])[0:1]
+            r = r + lax.dot_general(ones, hi, nt, preferred_element_type=F32) + lax.dot_general(ones, lo, nt, preferred_element_type=F32)
+        for i, (d, n) in enumerate(pairs):
+            m = i // 2 * TB
+            t = r[:, m : m + TB]
+            sqp[d, n] = pltpu.roll(t, TH, 1) if i % 2 else t
+
+    def k_step(pairs):
+        for d, n in pairs:
+            add_on(d, n, JK, kvp[target(d, n)], k_ring, zk, zkr)
+
+    def s_step(pairs):
+        for d, n in pairs:
+            add_on(d, n, JK, sqp[d, n], s_ring, sqs, sqr)
+
+    def q_step(pairs):
+        for d, n in pairs:
+            add_on(d, n, JQ, part[d, n], q_ring, zq, zqr)
+
+    me = (0, 0)
+    k_steps, q_steps = steps(JK), steps(JQ)
+    kvp[...] = sum(
+        jnp.dot(gath[:, f].reshape(NZ * TH, WIDTH), wcat[f, :, 0:HD], preferred_element_type=F32) for f in range(2)
+    ).reshape(NZ, TH, HD)
+    k_step(k_steps[0])
+    sq_product(k_steps[0])
+    s_step(k_steps[0])
+    cp_q.wait_recv()
+    cp_o.start()
+    q_weights(1)
+    q_product(q_steps[0])
+    q_step(q_steps[0])
+    for t in range(1, len(q_steps)):
+        last = t == len(q_steps) - 1
+        q_product(q_steps[t] + [me] * last)
+        if t < len(k_steps):
+            sq_product(k_steps[t] + [me] * (len(k_steps[t]) % 2))
+            k_step(k_steps[t])
+            s_step(k_steps[t])
+        q_step(q_steps[t])
+
+    squares = total(JK, sqp[me], s_ring, sqr)[0:1]
     squares = jnp.transpose(jnp.broadcast_to(squares, (HD, TB)))[0:TH]
     scale = lax.rsqrt(squares / MODEL + EPS)
 
@@ -292,22 +295,15 @@
     def kc_copy(d, xx):
         return rc(kvw.at[core, d, xx], kvw.at[core, d, xx], k_s, kc_r, dev_c)
 
-    k_ring(0, 7).wait_recv()
-    k_ring(1, 6).wait_recv()
-    kv = (part[7, TH:TB, 0:HD] + zkr[0, 7].astype(F32) + zkr[1, 6].astype(F32)) * scale
+    kv = total(JK, kvp[z], k_ring, zkr) * scale
     kvw[core, 0, xlo] = jnp.where(is_core0, rotated(kv), kv).astype(BF)
     for d in range(WIN - 1, 0, -1):
         k_copy(0, xlo, 0, at_z(d), d).start()
     k_copy(0, xlo, 1, dev_x).start()
     kc_copy(0, xlo).start()
 
-    queries = []
-    for p in range(2):
-        q_ring(0, 7, p).wait_recv()
-        q_ring(1, 6, p).wait_recv()
-        t = part[7, TH:TB, HD + p * QW : HD + p * QW + QW] + zqr[0, 7, p].astype(F32) + zqr[1, 6, p].astype(F32)
-        for j in range(2):
-            queries.append(rotated(t[:, HD * j : HD * (j + 1)] * scale).astype(BF))
+    q_sum = total(JQ, part[me], q_ring, zqr)
+    queries = [rotated(q_sum[:, HD * j : HD * (j + 1)] * scale).astype(BF) for j in range(4)]
     queries = jnp.concatenate(queries, axis=0)
 
     for d in range(1, WIN):
@@ -327,8 +323,8 @@
     tq = here + lax.broadcasted_iota(jnp.int32, (TH, KEYS), 0)
     allowed = (tk >= firsts(tq)) & (tk <= tq)
 
-    def d_copy(d, b, p):
-        return rc(att.at[b, p], att.at[b, p], d_s.at[d], d_r.at[b, p], at_z(1 - 2 * d))
+    def d_copy(d, b, p, hops=1):
+        return rc(att.at[b, p], att.at[b, p], d_s.at[d], d_r.at[b, p], at_z((1 - 2 * d) * hops))
 
     for j in range(4):
         sc = jnp.where(allowed, scores[TH * j : TH * (j + 1)], -1e30)
@@ -339,13 +335,15 @@
         if j % 2:
             for d in range(2):
                 d_copy(d, z, j // 2).start()
+                d_copy(d, z, j // 2, JK).start()
     cp_o.wait_recv()
 
-    def pass_on(d, k, b, last):
+    def pass_on(d, n):
+        b = zm(z - (1 - 2 * d) * n)
         for p in range(2):
             d_copy(d, b, p).wait_recv()
 
-            @pl.when(k < last)
+            @pl.when((n != JK - 1) & (n < 8 - d))
             def _():
                 d_copy(d, b, p).start()
 
@@ -396,12 +394,16 @@
                 es[m] = t.astype(BF)
                 e_copy(b, yb).start()
 
+    def hops(k):
+        odd = lax.rem(k, 2)
+        return odd * lax.div(k + 1, 2) + (1 - odd) * (JK - 1 + lax.div(k, 2))
+
+    def both(n):
+        return [zm(z - n), zm(z + n)]
+
     def gather_step(k, _):
-        pass_on(0, k, zm(z - k), 8)
-
-        @pl.when(k < 8)
-        def _():
-            pass_on(1, k, zm(z + k), 7)
+        for d in range(2):
+            pass_on(d, hops(k))
 
         @pl.when(k == 1)
         def _():
@@ -409,19 +411,32 @@
 
         @pl.when(k > 1)
         def _():
-            out_product([zm(z - k + 1), zm(z + k - 1)])
-            out_send(zm(z - k + 2))
+            out_product(both(hops(k - 1)))
+
+        @pl.when(k == 2)
+        def _():
+            out_send(z)
 
         @pl.when(k > 2)
         def _():
-            out_send(zm(z + k - 2))
+            for b in both(hops(k - 2)):
+                out_send(b)
 
         return 0
 
-    lax.fori_loop(1, 9, gather_step, 0)
+    lax.fori_loop(1, 7, gather_step, 0)
+    pass_on(0, 7)
+    pass_on(1, 7)
+    out_product(both(6))
+    for b in both(3):
+        out_send(b)
+    pass_on(0, 8)
+    out_product(both(7))
+    for b in both(6):
+        out_send(b)
     out_product([zm(z - 8)])
-    out_send(zm(z - 7))
-    out_send(zm(z + 7))
+    for b in both(7):
+        out_send(b)
     out_send(zm(z - 8))
 
     def y_sum(hh):
@@ -480,14 +495,15 @@
         v((2, WIDTH, WIDTH), BF),
         v((2, 1, WIDTH), F32),
         pltpu.SMEM((SEGS,), jnp.int32),
-        v((8, TB, COLS), F32),
-        v((2, 8, TH, HD), BF),
-        v((2, 8, TH, HD), BF),
-        v((2, 8, 2, TH, QW), BF),
-        v((2, 8, 2, TH, QW), BF),
-        v((8, 2, 8, TB), F32),
-        v((2, 8, 8, TB), F32),
-        v((2, 8, 8, TB), F32),
+        v((2, 9, TH, WIDTH), F32),
+        v((NZ, TH, HD), F32),
+        v((2, 9, TH, HD), BF),
+        v((2, 9, TH, HD), BF),
+        v((2, 9, TH, WIDTH), BF),
+        v((2, 9, TH, WIDTH), BF),
+        v((2, 9, 8, TB), F32),
+        v((2, 9, 8, TB), F32),
+        v((2, 9, 8, TB), F32),
         v((2, WIN, 2, TH, HD), BF),
         v((NZ, 2, TH, QW), BF),
         v((8, TH, 2 * WIDTH), BF),
@@ -501,9 +517,9 @@
         dma((6,)),
         dma, dma((12,)), dma,
         dma((4,)), dma((4,)),
-        dma((2,)), dma((2, 8)),
-        dma((2,)), dma((2, 8, 2)),
-        dma((2,)), dma((2, 8)),
+        dma((2,)), dma((2, 9)),
+        dma((2,)), dma((2, 9)),
+        dma((2,)), dma((2, 9)),
         dma, dma((WIN, 2)), dma,
         dma((2,)), dma((NZ, 2)),
         dma, dma((8,)),

time: 115 us -> 109 us (0.948)
  Pallas kernels: 113 us -> 107 us
    pallas_call x1, Pallas kernels: 113 us -> 107 us  [shards(): pl.pallas_call(body, name='attention_block', out_shape=jax.ShapeDtypeStru...]
where the time goes in v3:
time: 109 us
  Pallas kernels  107 us (98%)
  local copies, waits for them, and re-layouts  1.57 us (1%)
    pallas_call x1, Pallas kernels, shards(): pl.pallas_call(body, name='attention_block', out_shape=jax.ShapeDtypeStru...  107 us

profile of v3, /device:TPU:1, one launch (start us, length us, event | category | flops | bytes accessed | tf_op | source)
XLA Modules:
  0.0 109.1 jit_solution(13378567210842352963)
XLA Ops:
  0.0 107.5 %attention_block.1 = bf16[128,512]{1,0:T(8,128)(2,1)} custom-call(bf16[128,512]{1,0:T(8,128)(2,1)} %h.1, f32[1,512]{1,0:T(1,128)} %bitcast.1, bf16[512,512]{1,0:T(8,128)(2,1)} %wq.1, bf16[512,1024]{1,0:T(8,128)(2,1)} %wk.1, bf16[512,1024]{1,0:T(8,128)(2,1)} %wv.1, bf16[512,512]{1,0:T(8,128)(2,1)} %wo.1, s32[8]{0:T(128)} %seg.1), custom_call_target="tpu_custom_call" | custom-call | flops 3000000000 | bytes 3000000 | tf_op jit(solution)/shard_map/attention_block/pallas_call | solution.py:530
  107.5 1.6 %copy.9 = bf16[128,512]{1,0:T(8,128)(2,1)} copy(bf16[128,512]{1,0:T(8,128)(2,1)} %attention_block.1) | data formatting | bytes 262144

commit v4 on v3

--- a/solution.py
+++ b/solution.py
@@ -22,8 +22,11 @@
 WIDTH = 512
 QW = 256
 COLS = HD + WIDTH
-JK = 4
-JQ = 3
+JK = (4,)
+JQ = (3,)
+JD = (5,)
+ORDER = (1, 5, 2, 6, 3, 7, 4, 8)
+KROWS = TH + 16
 WIN = 5
 KEYS = WIN * TB
 MODEL = 16384
@@ -31,8 +34,8 @@
 
 def body(h, gain, wq, wk, wv, wo, seg, out, *s):
     (
-        gath, wraw, kvraw, wcat, wov, gv, segs, part, kvp, zk, zkr, zq, zqr, sqp, sqs, sqr, kvw, att, cs, cr, own, es, er, el, xs, xr,
-        in_sem, ga_s, ga_r, gc_r, w_s, w_r, zk_s, zk_r, zq_s, zq_r, q_s, q_r, k_s, k_r, kc_r, d_s, d_r, c_s, c_r, e_s, e_r, x_s, x_r,
+        gath, wraw, kvraw, wcat, wov, gv, segs, part, kvp, zk, zkr, zq, zqr, sqp, kvw, att, cs, cr, own, es, er, el, xs, xr,
+        in_sem, ga_s, ga_r, gc_r, w_s, w_r, zk_s, zk_r, zq_s, zq_r, k_s, k_r, kc_r, d_s, d_r, c_s, c_r, e_s, e_r, x_s, x_r,
     ) = s
     gx = lax.axis_index("gx")
     gy = lax.axis_index("gy")
@@ -46,8 +49,8 @@
     def ym(v):
         return lax.rem(v + 4, 4)
 
-    def at_z(d):
-        return {"gx": xlo * NZ + zm(z + d), "gy": gy}
+    def at_z(d, xx=None):
+        return {"gx": (xlo if xx is None else xx) * NZ + zm(z + d), "gy": gy}
 
     def at_y(yy):
         return {"gx": gx, "gy": xhi * 8 + yy * 2 + core}
@@ -65,7 +68,7 @@
         return pltpu.make_async_remote_copy(src_ref=src, dst_ref=dst, send_sem=ss, recv_sem=rs, device_id=dev, device_id_type=MESH)
 
     barrier = pltpu.get_barrier_semaphore()
-    greet = [dev_x, dev_h, dev_d, dev_c] + [at_y(ym(y + d)) for d in (1, 2, 3)] + [at_z(d) for d in (1, 2, 3, 4, -1, -2, -3, -4)]
+    greet = [dev_x, dev_h, dev_d, dev_c] + [at_y(ym(y + d)) for d in (1, 2, 3)] + [at_z(d) for d in (1, 2, 3, 4, 5, -1, -2, -3, -4, -5)]
     for d in greet:
         pl.semaphore_signal(barrier, inc=1, device_id=d, device_id_type=MESH)
     is_core0 = core == 0
@@ -114,8 +117,8 @@
         g_copy(gath.at[gy, 0], at[d], at_y(ym(y + d)), h.at[mine]).start()
 
     cp_g = rc(gain, gv.at[1], w_s.at[1], w_r.at[1], dev_x)
-    cp_q = rc(wq, wraw.at[1], w_s.at[2], w_r.at[2], dev_x)
-    cp_o = rc(wo, wov.at[1], w_s.at[3], w_r.at[3], dev_x)
+    cp_q = [rc(wq.at[:, pl.ds(p * QW, QW)], wraw.at[1, :, pl.ds(p * QW, QW)], w_s.at[2 + p], w_r.at[2 + p], dev_x) for p in range(2)]
+    cp_o = rc(wo, wov.at[1], w_s.at[4], w_r.at[4], dev_x)
     cp_g.start()
     rc(h.at[mine], gath.at[gy, 0], ga_s, gc_r, dev_c).start()
 
@@ -129,9 +132,9 @@
     def kv_weights(f):
         wcat[f, :, 0:HD] = (kvraw[f].astype(F32) * gain_column(f)).astype(BF)
 
-    def q_weights(f):
+    def q_weights(f, p):
         col = gain_column(f)
-        for j in range(WIDTH // HD):
+        for j in range(2 * p, 2 * p + 2):
             wcat[f, :, HD * (j + 1) : HD * (j + 2)] = (wraw[f, :, HD * j : HD * (j + 1)].astype(F32) * col).astype(BF)
 
     g_copy(gath.at[gy, 1], 0, dev_x).wait_recv()
@@ -151,9 +154,10 @@
     def _():
         kv_send(wv).start()
 
-    cp_q.start()
+    cp_q[0].start()
     kv_weights(0)
-    q_weights(0)
+    for p in range(2):
+        q_weights(0, p)
 
     def firsts(tq):
         start = jnp.zeros_like(tq)
@@ -181,50 +185,49 @@
         g_copy(gath.at[b, 0], by[d], dev_c).wait_recv()
         g_copy(gath.at[b, 1], by[d] + 1, dev_c).wait_recv()
         gc_copy(gath.at[b]).start()
+    rc(kvraw.at[0], kvraw.at[1], w_s.at[0], w_r.at[0], dev_x).wait_recv()
+    cp_q[1].start()
+    cp_g.wait_recv()
+    kv_weights(1)
     for d in ys:
         b = blk(hot, ym(y + d), core)
         g_copy(gath.at[b], by[d] + 2, dev_c).wait_recv()
         gc_copy(gath.at[b]).start()
-    rc(kvraw.at[0], kvraw.at[1], w_s.at[0], w_r.at[0], dev_x).wait_recv()
-    cp_g.wait_recv()
-    kv_weights(1)
     gc_copy(gath.at[pl.ds(0, 8)]).wait_recv()
 
     ones = jnp.ones((8, WIDTH), BF)
     nt = (((1,), (1,)), ((), ()))
 
-    def steps(j):
-        heads = [(0, 8), (0, j - 1), (1, 7), (1, j - 1)]
-        ends = [j, 1, j, 1]
-        return [[(d, n - t) for (d, n), e in zip(heads, ends) if n - t >= e] for t in range(9 - j)]
+    def steps(jumps):
+        ends = (*jumps, 1)
+        runs = [(d, top, end) for d in range(2) for top, end in zip((8 - d, *(j - 1 for j in jumps)), ends)]
+        most = max(top - end for _, top, end in runs) + 1
+        return [[(d, top - t) for d, top, end in runs if top - t >= end] for t in range(most)]
 
     def target(d, n):
         return zm(z + (1 - 2 * d) * n)
 
-    def leg(d, n, j):
-        return at_z((1 - 2 * d) * (j if n == j else 1))
+    def leg(d, n, jumps):
+        return at_z((1 - 2 * d) * (n if n in jumps else 1))
 
     def k_ring(d, n):
         return rc(zk.at[d, n], zkr.at[d, n], zk_s.at[d], zk_r.at[d, n], leg(d, n, JK))
 
-    def q_ring(d, n):
-        return rc(zq.at[d, n], zqr.at[d, n], zq_s.at[d], zq_r.at[d, n], leg(d, n, JQ))
-
-    def s_ring(d, n):
-        return rc(sqs.at[d, n], sqr.at[d, n], q_s.at[d], q_r.at[d, n], leg(d, n, JK))
-
-    def add_on(d, n, j, mine, ring, stage, got):
-        t = mine
-        if n + 1 <= 8 - d and n + 1 != j:
-            ring(d, n + 1).wait_recv()
-            t = t + got[d, n + 1].astype(F32)
-        stage[d, n] = t.astype(stage.dtype)
-        ring(d, n).start()
-
-    def total(j, mine, ring, got):
+    def q_ring(p):
+        return lambda d, n: rc(zq.at[p, d, n], zqr.at[p, d, n], zq_s.at[p, d], zq_r.at[p, d, n], leg(d, n, JQ))
+
+    def before(d, n, jumps):
+        return n + 1 <= 8 - d and n + 1 not in jumps
+
+    def read_kv(d, n):
+        k_ring(d, n).wait_recv()
+        v = zkr[d, n].astype(F32)
+        return v[0:TH], v[TH : TH + 8] + v[TH + 8 :]
+
+    def total(jumps, mine, ring, got):
         t = mine
         for d in range(2):
-            for n in (1, j):
+            for n in (1, *jumps):
                 ring(d, n).wait_recv()
                 t = t + got[d, n].astype(F32)
         return t
@@ -232,10 +235,11 @@
     def rows_of(pairs, f):
         return jnp.concatenate([gath[target(d, n), f] for d, n in pairs], axis=0)
 
-    def q_product(pairs):
-        res = sum(jnp.dot(rows_of(pairs, f), wcat[f, :, HD:], preferred_element_type=F32) for f in range(2))
+    def q_product(p, pairs):
+        cols = slice(HD + p * QW, HD + p * QW + QW)
+        res = sum(jnp.dot(rows_of(pairs, f), wcat[f, :, cols], preferred_element_type=F32) for f in range(2))
         for i, (d, n) in enumerate(pairs):
-            part[d, n] = res[i * TH : i * TH + TH]
+            part[p, d, n] = res[i * TH : i * TH + TH]
 
     def sq_product(pairs):
         r = jnp.zeros((8, len(pairs) * TH), F32)
@@ -252,42 +256,30 @@
 
     def k_step(pairs):
         for d, n in pairs:
-            add_on(d, n, JK, kvp[target(d, n)], k_ring, zk, zkr)
-
-    def s_step(pairs):
+            t, q = kvp[target(d, n)], sqp[d, n]
+            if before(d, n, JK):
+                t2, q2 = read_kv(d, n + 1)
+                t, q = t + t2, q + q2
+            hi = q.astype(BF).astype(F32)
+            zk[d, n] = jnp.concatenate([t, hi, q - hi], axis=0).astype(BF)
+            k_ring(d, n).start()
+
+    def q_step(p, pairs):
         for d, n in pairs:
-            add_on(d, n, JK, sqp[d, n], s_ring, sqs, sqr)
-
-    def q_step(pairs):
-        for d, n in pairs:
-            add_on(d, n, JQ, part[d, n], q_ring, zq, zqr)
+            t = part[p, d, n]
+            if before(d, n, JQ):
+                q_ring(p)(d, n + 1).wait_recv()
+                t = t + zqr[p, d, n + 1].astype(F32)
+            zq[p, d, n] = t.astype(BF)
+            q_ring(p)(d, n).start()
 
     me = (0, 0)
     k_steps, q_steps = steps(JK), steps(JQ)
     kvp[...] = sum(
         jnp.dot(gath[:, f].reshape(NZ * TH, WIDTH), wcat[f, :, 0:HD], preferred_element_type=F32) for f in range(2)
     ).reshape(NZ, TH, HD)
+    sq_product(k_steps[0])
     k_step(k_steps[0])
-    sq_product(k_steps[0])
-    s_step(k_steps[0])
-    cp_q.wait_recv()
-    cp_o.start()
-    q_weights(1)
-    q_product(q_steps[0])
-    q_step(q_steps[0])
-    for t in range(1, len(q_steps)):
-        last = t == len(q_steps) - 1
-        q_product(q_steps[t] + [me] * last)
-        if t < len(k_steps):
-            sq_product(k_steps[t] + [me] * (len(k_steps[t]) % 2))
-            k_step(k_steps[t])
-            s_step(k_steps[t])
-        q_step(q_steps[t])
-
-    squares = total(JK, sqp[me], s_ring, sqr)[0:1]
-    squares = jnp.transpose(jnp.broadcast_to(squares, (HD, TB)))[0:TH]
-    scale = lax.rsqrt(squares / MODEL + EPS)
-
     def k_copy(d, xx, n, dev, dd=None):
         to = d if dd is None else dd
         return rc(kvw.at[core, d, xx], kvw.at[core, to, xx], k_s, k_r.at[to, n], dev)
@@ -295,24 +287,58 @@
     def kc_copy(d, xx):
         return rc(kvw.at[core, d, xx], kvw.at[core, d, xx], k_s, kc_r, dev_c)
 
-    kv = total(JK, kvp[z], k_ring, zkr) * scale
-    kvw[core, 0, xlo] = jnp.where(is_core0, rotated(kv), kv).astype(BF)
-    for d in range(WIN - 1, 0, -1):
-        k_copy(0, xlo, 0, at_z(d), d).start()
-    k_copy(0, xlo, 1, dev_x).start()
-    kc_copy(0, xlo).start()
-
-    q_sum = total(JQ, part[me], q_ring, zqr)
-    queries = [rotated(q_sum[:, HD * j : HD * (j + 1)] * scale).astype(BF) for j in range(4)]
-    queries = jnp.concatenate(queries, axis=0)
-
+    def window_sends():
+        kv, squares = kvp[z], sqp[me]
+        for d in range(2):
+            for n in (1, *JK):
+                t, q = read_kv(d, n)
+                kv, squares = kv + t, squares + q
+        squares = jnp.transpose(jnp.broadcast_to(squares[0:1], (HD, TB)))[0:TH]
+        scale = lax.rsqrt(squares / MODEL + EPS)
+        kv = kv * scale
+        kvw[core, 0, xlo] = jnp.where(is_core0, rotated(kv), kv).astype(BF)
+        for d in range(WIN - 1, 0, -1):
+            k_copy(0, xlo, 0, at_z(d), d).start()
+        k_copy(0, xlo, 1, dev_x).start()
+        kc_copy(0, xlo).start()
+        return scale
+
+    def queries_of(p):
+        t = total(JQ, part[(p, *me)], q_ring(p), zqr.at[p])
+        return [rotated(t[:, HD * j : HD * (j + 1)] * scale).astype(BF) for j in range(2)]
+
+    lag = 1
+    n_q = len(q_steps)
+    for t in range(n_q + lag):
+        if t == 0:
+            cp_q[0].wait_recv()
+            q_weights(1, 0)
+        if t == lag:
+            cp_q[1].wait_recv()
+            cp_o.start()
+            q_weights(1, 1)
+        now = [(p, t - p * lag) for p in range(2) if 0 <= t - p * lag < n_q]
+        for p, i in now:
+            q_product(p, q_steps[i] + [me] * (i == n_q - 1))
+        if 0 < t < len(k_steps):
+            sq_product(k_steps[t] + [me] * (len(k_steps[t]) % 2))
+            k_step(k_steps[t])
+        for p, i in now:
+            q_step(p, q_steps[i])
+        if t == len(k_steps):
+            scale = window_sends()
+
+    queries = queries_of(0)
+    k_copy(0, xot, 1, dev_x).wait_recv()
+    kc_copy(0, xot).start()
     for d in range(1, WIN):
         k_copy(d, xlo, 0, dev_x).wait_recv()
         k_copy(d, xlo, 1, dev_x).start()
         kc_copy(d, xlo).start()
-    for d in range(WIN):
+    for d in range(1, WIN):
         k_copy(d, xot, 1, dev_x).wait_recv()
         kc_copy(d, xot).start()
+    queries = jnp.concatenate(queries + queries_of(1), axis=0)
     rc(kvw.at[cot], kvw.at[cot], k_s, kc_r, dev_c).wait_recv()
 
     keys = kvw[0].reshape(KEYS, HD)
@@ -334,17 +360,16 @@
         att[z, j // 2, :, HD * (j % 2) : HD * (j % 2 + 1)] = o.astype(BF)
         if j % 2:
             for d in range(2):
+                for hops in JD:
+                    d_copy(d, z, j // 2, hops).start()
                 d_copy(d, z, j // 2).start()
-                d_copy(d, z, j // 2, JK).start()
     cp_o.wait_recv()
 
     def pass_on(d, n):
         b = zm(z - (1 - 2 * d) * n)
         for p in range(2):
             d_copy(d, b, p).wait_recv()
-
-            @pl.when((n != JK - 1) & (n < 8 - d))
-            def _():
+            if n + 1 not in JD and n < 8 - d:
                 d_copy(d, b, p).start()
 
     def c_copy(b):
@@ -394,50 +419,19 @@
                 es[m] = t.astype(BF)
                 e_copy(b, yb).start()
 
-    def hops(k):
-        odd = lax.rem(k, 2)
-        return odd * lax.div(k + 1, 2) + (1 - odd) * (JK - 1 + lax.div(k, 2))
-
     def both(n):
-        return [zm(z - n), zm(z + n)]
-
-    def gather_step(k, _):
-        for d in range(2):
-            pass_on(d, hops(k))
-
-        @pl.when(k == 1)
-        def _():
-            out_product([z])
-
-        @pl.when(k > 1)
-        def _():
-            out_product(both(hops(k - 1)))
-
-        @pl.when(k == 2)
-        def _():
-            out_send(z)
-
-        @pl.when(k > 2)
-        def _():
-            for b in both(hops(k - 2)):
+        return [zm(z - n), zm(z + n)][: 1 if n in (0, 8) else 2]
+
+    done = (0, *ORDER)
+    for i in range(1, 11):
+        if i < 9:
+            for d in range(2 if done[i] < 8 else 1):
+                pass_on(d, done[i])
+        if i < 10:
+            out_product(both(done[i - 1]))
+        if i > 1:
+            for b in both(done[i - 2]):
                 out_send(b)
-
-        return 0
-
-    lax.fori_loop(1, 7, gather_step, 0)
-    pass_on(0, 7)
-    pass_on(1, 7)
-    out_product(both(6))
-    for b in both(3):
-        out_send(b)
-    pass_on(0, 8)
-    out_product(both(7))
-    for b in both(6):
-        out_send(b)
-    out_product([zm(z - 8)])
-    for b in both(7):
-        out_send(b)
-    out_send(zm(z - 8))
 
     def y_sum(hh):
         t = el[hh]
@@ -471,12 +465,13 @@
     left(pieces.at[pl.ds(0, 31)], ga_s)
     left(kvraw.at[0], w_s.at[0])
     cp_g.wait_send()
-    cp_q.wait_send()
+    for c in cp_q:
+        c.wait_send()
     cp_o.wait_send()
     for d in range(2):
         left(zk.at[d, pl.ds(0, 8 - d)], zk_s.at[d])
-        left(zq.at[d, pl.ds(0, 8 - d)], zq_s.at[d])
-        left(sqs.at[d, pl.ds(0, 8 - d)], q_s.at[d])
+        for p in range(2):
+            left(zq.at[p, d, pl.ds(0, 8 - d)], zq_s.at[p, d])
         left(att.at[pl.ds(0, 8 - d)], d_s.at[d])
     left(kvw.reshape(4 * WIN, TH, HD).at[pl.ds(0, 4 * WIN - 1)], k_s)
     left(cs, c_s)
@@ -495,14 +490,12 @@
         v((2, WIDTH, WIDTH), BF),
         v((2, 1, WIDTH), F32),
         pltpu.SMEM((SEGS,), jnp.int32),
-        v((2, 9, TH, WIDTH), F32),
+        v((2, 2, 9, TH, QW), F32),
         v((NZ, TH, HD), F32),
-        v((2, 9, TH, HD), BF),
-        v((2, 9, TH, HD), BF),
-        v((2, 9, TH, WIDTH), BF),
-        v((2, 9, TH, WIDTH), BF),
-        v((2, 9, 8, TB), F32),
-        v((2, 9, 8, TB), F32),
+        v((2, 9, KROWS, HD), BF),
+        v((2, 9, KROWS, HD), BF),
+        v((2, 2, 9, TH, QW), BF),
+        v((2, 2, 9, TH, QW), BF),
         v((2, 9, 8, TB), F32),
         v((2, WIN, 2, TH, HD), BF),
         v((NZ, 2, TH, QW), BF),
@@ -516,10 +509,9 @@
         v((3, TH, WIDTH), BF),
         dma((6,)),
         dma, dma((12,)), dma,
-        dma((4,)), dma((4,)),
+        dma((5,)), dma((5,)),
         dma((2,)), dma((2, 9)),
-        dma((2,)), dma((2, 9)),
-        dma((2,)), dma((2, 9)),
+        dma((2, 2)), dma((2, 2, 9)),
         dma, dma((WIN, 2)), dma,
         dma((2,)), dma((NZ, 2)),
         dma, dma((8,)),

time: 109 us -> 101 us (0.927)
  Pallas kernels: 107 us -> 99 us
    pallas_call x1, Pallas kernels: 107 us -> 99 us  [shards(): pl.pallas_call(body, name='attention_block', out_shape=jax.ShapeDtypeStru...]
where the time goes in v4:
time: 101 us
  Pallas kernels  99 us (98%)
  local copies, waits for them, and re-layouts  1.57 us (2%)
    pallas_call x1, Pallas kernels, shards(): pl.pallas_call(body, name='attention_block', out_shape=jax.ShapeDtypeStru...  99 us

profile of v4, /device:TPU:1, one launch (start us, length us, event | category | flops | bytes accessed | tf_op | source)
XLA Modules:
  0.0 100.6 jit_solution(5563370550990120756)
XLA Ops:
  0.0 99.0 %attention_block.1 = bf16[128,512]{1,0:T(8,128)(2,1)} custom-call(bf16[128,512]{1,0:T(8,128)(2,1)} %h.1, f32[1,512]{1,0:T(1,128)} %bitcast.1, bf16[512,512]{1,0:T(8,128)(2,1)} %wq.1, bf16[512,1024]{1,0:T(8,128)(2,1)} %wk.1, bf16[512,1024]{1,0:T(8,128)(2,1)} %wv.1, bf16[512,512]{1,0:T(8,128)(2,1)} %wo.1, s32[8]{0:T(128)} %seg.1), custom_call_target="tpu_custom_call" | custom-call | flops 3000000000 | bytes 3000000 | tf_op jit(solution)/shard_map/attention_block/pallas_call | solution.py:522
  99.0 1.6 %copy.9 = bf16[128,512]{1,0:T(8,128)(2,1)} copy(bf16[128,512]{1,0:T(8,128)(2,1)} %attention_block.1) | data formatting | bytes 262144

commit v5 on v4

--- a/solution.py
+++ b/solution.py
@@ -22,8 +22,8 @@
 WIDTH = 512
 QW = 256
 COLS = HD + WIDTH
-JK = (4,)
-JQ = (3,)
+JK = (5,)
+JQ = (4,)
 JD = (5,)
 ORDER = (1, 5, 2, 6, 3, 7, 4, 8)
 KROWS = TH + 16
@@ -107,7 +107,7 @@
     def gc_copy(ref):
         return rc(ref, ref, ga_s, gc_r, dev_c)
 
-    ys = (1, 3, 2)
+    ys = (2, 1, 3)
     at = {1: 4, 3: 1, 2: 7}
     by = {1: 1, 3: 4, 2: 7}
     g_copy(gath.at[gy, 1], 0, dev_x, h.at[other]).start()
@@ -201,6 +201,7 @@
     def steps(jumps):
         ends = (*jumps, 1)
         runs = [(d, top, end) for d in range(2) for top, end in zip((8 - d, *(j - 1 for j in jumps)), ends)]
+        runs.sort(key=lambda r: -r[1])
         most = max(top - end for _, top, end in runs) + 1
         return [[(d, top - t) for d, top, end in runs if top - t >= end] for t in range(most)]
 
@@ -245,10 +246,7 @@
         r = jnp.zeros((8, len(pairs) * TH), F32)
         for f in range(2):
             xf = rows_of(pairs, f).astype(F32)
-            x2 = xf * xf
-            hi = x2.astype(BF)
-            lo = (x2 - hi.astype(F32)).astype(BF)
-            r = r + lax.dot_general(ones, hi, nt, preferred_element_type=F32) + lax.dot_general(ones, lo, nt, preferred_element_type=F32)
+            r = r + lax.dot_general(ones, (xf * xf).astype(BF), nt, preferred_element_type=F32)
         for i, (d, n) in enumerate(pairs):
             m = i // 2 * TB
             t = r[:, m : m + TB]
@@ -256,7 +254,7 @@
 
     def k_step(pairs):
         for d, n in pairs:
-            t, q = kvp[target(d, n)], sqp[d, n]
+            t, q = kvp[d, n], sqp[d, n]
             if before(d, n, JK):
                 t2, q2 = read_kv(d, n + 1)
                 t, q = t + t2, q + q2
@@ -275,9 +273,12 @@
 
     me = (0, 0)
     k_steps, q_steps = steps(JK), steps(JQ)
-    kvp[...] = sum(
-        jnp.dot(gath[:, f].reshape(NZ * TH, WIDTH), wcat[f, :, 0:HD], preferred_element_type=F32) for f in range(2)
-    ).reshape(NZ, TH, HD)
+    def kv_product(pairs):
+        res = sum(jnp.dot(rows_of(pairs, f), wcat[f, :, 0:HD], preferred_element_type=F32) for f in range(2))
+        for i, (d, n) in enumerate(pairs):
+            kvp[d, n] = res[i * TH : i * TH + TH]
+
+    kv_product(k_steps[0])
     sq_product(k_steps[0])
     k_step(k_steps[0])
     def k_copy(d, xx, n, dev, dd=None):
@@ -288,7 +289,7 @@
         return rc(kvw.at[core, d, xx], kvw.at[core, d, xx], k_s, kc_r, dev_c)
 
     def window_sends():
-        kv, squares = kvp[z], sqp[me]
+        kv, squares = kvp[me], sqp[me]
         for d in range(2):
             for n in (1, *JK):
                 t, q = read_kv(d, n)
@@ -307,7 +308,7 @@
         t = total(JQ, part[(p, *me)], q_ring(p), zqr.at[p])
         return [rotated(t[:, HD * j : HD * (j + 1)] * scale).astype(BF) for j in range(2)]
 
-    lag = 1
+    lag = 2
     n_q = len(q_steps)
     for t in range(n_q + lag):
         if t == 0:
@@ -321,7 +322,9 @@
         for p, i in now:
             q_product(p, q_steps[i] + [me] * (i == n_q - 1))
         if 0 < t < len(k_steps):
-            sq_product(k_steps[t] + [me] * (len(k_steps[t]) % 2))
+            pairs = k_steps[t] + [me] * (t == len(k_steps) - 1)
+            kv_product(pairs)
+            sq_product(pairs)
             k_step(k_steps[t])
         for p, i in now:
             q_step(p, q_steps[i])
@@ -427,9 +430,12 @@
         if i < 9:
             for d in range(2 if done[i] < 8 else 1):
                 pass_on(d, done[i])
+        if 1 < i < 9:
+            for b in both(done[i - 2]):
+                out_send(b)
         if i < 10:
             out_product(both(done[i - 1]))
-        if i > 1:
+        if i > 8:
             for b in both(done[i - 2]):
                 out_send(b)
 
@@ -491,7 +497,7 @@
         v((2, 1, WIDTH), F32),
         pltpu.SMEM((SEGS,), jnp.int32),
         v((2, 2, 9, TH, QW), F32),
-        v((NZ, TH, HD), F32),
+        v((2, 9, TH, HD), F32),
         v((2, 9, KROWS, HD), BF),
         v((2, 9, KROWS, HD), BF),
         v((2, 2, 9, TH, QW), BF),

time: 101 us -> 101 us (level)
  the two profiles are of different devices: /device:TPU:1 before, /device:TPU:33 now
where the time goes in v5:
time: 101 us; the launch traced here: 100 us
  Pallas kernels  98.8 us (98%)
  local copies, waits for them, and re-layouts  1.57 us (2%)
    pallas_call x1, Pallas kernels, shards(): pl.pallas_call(body, name='attention_block', out_shape=jax.ShapeDtypeStru...  98.8 us

profile of v5, /device:TPU:33, one launch (start us, length us, event | category | flops | bytes accessed | tf_op | source)
XLA Modules:
  0.0 100.4 jit_solution(15842505524669543379)
XLA Ops:
  0.0 98.8 %attention_block.1 = bf16[128,512]{1,0:T(8,128)(2,1)} custom-call(bf16[128,512]{1,0:T(8,128)(2,1)} %h.1, f32[1,512]{1,0:T(1,128)} %bitcast.1, bf16[512,512]{1,0:T(8,128)(2,1)} %wq.1, bf16[512,1024]{1,0:T(8,128)(2,1)} %wk.1, bf16[512,1024]{1,0:T(8,128)(2,1)} %wv.1, bf16[512,512]{1,0:T(8,128)(2,1)} %wo.1, s32[8]{0:T(128)} %seg.1), custom_call_target="tpu_custom_call" | custom-call | flops 3000000000 | bytes 3000000 | tf_op jit(solution)/shard_map/attention_block/pallas_call | solution.py:528
  98.8 1.6 %copy.9 = bf16[128,512]{1,0:T(8,128)(2,1)} copy(bf16[128,512]{1,0:T(8,128)(2,1)} %attention_block.1) | data formatting | bytes 262144

commit v6 on v5

--- a/solution.py
+++ b/solution.py
@@ -109,6 +109,8 @@
 
     ys = (2, 1, 3)
     at = {1: 4, 3: 1, 2: 7}
+    at2 = {1: 13, 3: 12, 2: 14}
+    by2 = {1: 12, 3: 13, 2: 14}
     by = {1: 1, 3: 4, 2: 7}
     g_copy(gath.at[gy, 1], 0, dev_x, h.at[other]).start()
     g_copy(gath.at[gy, 0], 10, dev_h, h.at[mine]).start()
@@ -137,15 +139,18 @@
         for j in range(2 * p, 2 * p + 2):
             wcat[f, :, HD * (j + 1) : HD * (j + 2)] = (wraw[f, :, HD * j : HD * (j + 1)].astype(F32) * col).astype(BF)
 
+    g_copy(gath.at[far, 1], 11, dev_d).wait_recv()
+    for d in ys:
+        g_copy(gath.at[far, 1], at2[d], at_y(ym(y + d))).start()
+    gc_copy(gath.at[far, 1]).start()
     g_copy(gath.at[gy, 1], 0, dev_x).wait_recv()
     for d in ys:
         g_copy(gath.at[gy, 1], at[d] + 1, at_y(ym(y + d))).start()
     gc_copy(gath.at[gy, 1]).start()
     g_copy(gath.at[far, 0], 10, dev_h).wait_recv()
-    g_copy(gath.at[far, 1], 11, dev_d).wait_recv()
     for d in ys:
-        g_copy(gath.at[far], at[d] + 2, at_y(ym(y + d))).start()
-    gc_copy(gath.at[far]).start()
+        g_copy(gath.at[far, 0], at[d] + 2, at_y(ym(y + d))).start()
+    gc_copy(gath.at[far, 0]).start()
     @pl.when(is_core0)
     def _():
         kv_send(wk).start()
@@ -154,7 +159,8 @@
     def _():
         kv_send(wv).start()
 
-    cp_q[0].start()
+    for c in cp_q:
+        c.start()
     kv_weights(0)
     for p in range(2):
         q_weights(0, p)
@@ -185,14 +191,14 @@
         g_copy(gath.at[b, 0], by[d], dev_c).wait_recv()
         g_copy(gath.at[b, 1], by[d] + 1, dev_c).wait_recv()
         gc_copy(gath.at[b]).start()
+    for d in ys:
+        b = blk(hot, ym(y + d), core)
+        g_copy(gath.at[b, 1], by2[d], dev_c).wait_recv()
+        g_copy(gath.at[b, 0], by[d] + 2, dev_c).wait_recv()
+        gc_copy(gath.at[b]).start()
     rc(kvraw.at[0], kvraw.at[1], w_s.at[0], w_r.at[0], dev_x).wait_recv()
-    cp_q[1].start()
     cp_g.wait_recv()
     kv_weights(1)
-    for d in ys:
-        b = blk(hot, ym(y + d), core)
-        g_copy(gath.at[b], by[d] + 2, dev_c).wait_recv()
-        gc_copy(gath.at[b]).start()
     gc_copy(gath.at[pl.ds(0, 8)]).wait_recv()
 
     ones = jnp.ones((8, WIDTH), BF)
@@ -514,7 +520,7 @@
         v((3, TH, WIDTH), BF),
         v((3, TH, WIDTH), BF),
         dma((6,)),
-        dma, dma((12,)), dma,
+        dma, dma((15,)), dma,
         dma((5,)), dma((5,)),
         dma((2,)), dma((2, 9)),
         dma((2, 2)), dma((2, 2, 9)),

time: 101 us -> 101 us (level)
  the two profiles are of different devices: /device:TPU:33 before, /device:TPU:32 now
where the time goes in v6:
time: 101 us; the launch traced here: 100 us
  Pallas kernels  98.9 us (98%)
  local copies, waits for them, and re-layouts  1.57 us (2%)
    pallas_call x1, Pallas kernels, shards(): pl.pallas_call(body, name='attention_block', out_shape=jax.ShapeDtypeStru...  98.9 us

profile of v6, /device:TPU:32, one launch (start us, length us, event | category | flops | bytes accessed | tf_op | source)
XLA Modules:
  0.0 100.5 jit_solution(18268360457197983656)
XLA Ops:
  0.0 98.9 %attention_block.1 = bf16[128,512]{1,0:T(8,128)(2,1)} custom-call(bf16[128,512]{1,0:T(8,128)(2,1)} %h.1, f32[1,512]{1,0:T(1,128)} %bitcast.1, bf16[512,512]{1,0:T(8,128)(2,1)} %wq.1, bf16[512,1024]{1,0:T(8,128)(2,1)} %wk.1, bf16[512,1024]{1,0:T(8,128)(2,1)} %wv.1, bf16[512,512]{1,0:T(8,128)(2,1)} %wo.1, s32[8]{0:T(128)} %seg.1), custom_call_target="tpu_custom_call" | custom-call | flops 3000000000 | bytes 3000000 | tf_op jit(solution)/shard_map/attention_block/pallas_call | solution.py:534
  98.9 1.6 %copy.9 = bf16[128,512]{1,0:T(8,128)(2,1)} copy(bf16[128,512]{1,0:T(8,128)(2,1)} %attention_block.1) | data formatting | bytes 262144
